TPU v7x, 256 devices: a whole 4x4x8 slice. The times are simulated.
256 devices in a mesh: kv: 32 (over y, x, core), head: 8 (over z).
Axes of the slice: x: 4, y: 4, z: 8, core: 2. Of those that a mesh axis runs over, the one named last changes fastest.
Arguments:
- queries: bfloat16 [32, 128, 128], P('head', 'kv'), as said below
- keys: bfloat16 [8, 393216, 128], P('head', 'kv'), as said below
- values: bfloat16 [8, 393216, 128], P('head', 'kv'), may hold values from -6 to 6
- step_keys: bfloat16 [2, 16, 8, 128], P(None, None, 'head'), may hold values from -15 to 15
- step_values: bfloat16 [2, 16, 8, 128], P(None, None, 'head'), may hold values from -6 to 6
- lengths: int32 [16], replicated, may hold values from 6400 to 98304, as said below
- block_table: int32 [2, 1536], P(None, 'kv'), may hold values from -1 to 383, as said below
Outputs:
- attended: float32 [32, 128, 128], P('head', 'kv')
Inputs may be any that keep to these rules, and one draw needn't show every extreme that they name: `lengths`: one sequence has exactly 98304 tokens; every other has 6400 to 19200. `block_table`: row 0 names a block's sequence or -1; row 1 its block number (0 where unused). Every block number 0 to ceil(lengths[r] / 256) - 1 of every sequence r stands in exactly one column, and some columns are unused. `queries`: values lie in -15 to 15. `keys`: values lie in -6 to 6.
All inputs are finite; a program needn't handle non-finite values.
Results may differ from a plain program's by a relative error of at most 0.02075.
Values may be sent and summed in bfloat16 or wider, within the bound.
No kernel may reach another device: no remote copies, remote signals or barrier semaphores. Data moves between devices by JAX's collectives and lax.ppermute only.
A program may use at most 64 MiB of HBM per device.

v0:
```python
import math

import jax
import jax.numpy as jnp
from jax import lax
from jax.sharding import PartitionSpec as P

QUERY_HEAD_COUNT = 128
KEY_VALUE_HEADS = 8


lowest = -1e30


def on_device(queries, keys, values, step_keys, step_values, lengths, block_table):
    steps_count = step_keys.shape[0]
    rows_count = step_keys.shape[1]
    kv_local = keys.shape[0]
    head_size = keys.shape[2]
    query_group = QUERY_HEAD_COUNT // KEY_VALUE_HEADS
    slots = block_table.shape[1]
    block_len = keys.shape[1] // slots
    rescale_factor = 1.0 / math.sqrt(head_size)
    wide = lax.all_gather(queries, "kv", axis=1, tiled=True)
    every = lax.all_gather(wide, "head", axis=0, tiled=True)
    first_head = lax.axis_index("head") * (kv_local * query_group)
    own = lax.dynamic_slice_in_dim(every, first_head, kv_local * query_group, 1)
    own = own.reshape(steps_count, rows_count, kv_local, query_group, head_size).transpose(
        2, 0, 1, 3, 4
    )
    row_ids = block_table[0]
    block_ids = block_table[1]
    row_safe = jnp.clip(row_ids, 0, rows_count - 1)
    selected_slots = jnp.take(own, row_safe, axis=2).transpose(0, 2, 1, 3, 4)
    selected_slots = selected_slots.reshape(kv_local, slots, steps_count * query_group, head_size)
    paged_key_blocks = keys.reshape(kv_local, slots, block_len, head_size)
    paged_value_blocks = values.reshape(kv_local, slots, block_len, head_size)
    attention_scores = (
        jnp.einsum(
            "kbqd,kbtd->kbqt", selected_slots, paged_key_blocks, preferred_element_type=jnp.float32
        )
        * rescale_factor
    )
    offsets = block_ids[:, None] * block_len + jnp.arange(block_len, dtype=jnp.int32)[None, :]
    valid = (row_ids[:, None] >= 0) & (offsets < jnp.take(lengths, row_safe)[:, None])
    attention_scores = jnp.where(valid[None, :, None, :], attention_scores, lowest)
    member = row_ids[:, None] == jnp.arange(rows_count, dtype=jnp.int32)[None, :]
    slot_max = jnp.max(attention_scores, axis=-1)
    row_max = jnp.max(jnp.where(member[None, :, :, None], slot_max[:, :, None, :], lowest), axis=1)
    new_scores = (
        jnp.einsum("ksrgd,trkd->krsgt", own, step_keys, preferred_element_type=jnp.float32)
        * rescale_factor
    )
    causal = (jnp.arange(steps_count)[None, :] <= jnp.arange(steps_count)[:, None]) & (
        lax.axis_index("kv") == 0
    )
    mask_new = jnp.broadcast_to(causal[None, None, :, None, :], new_scores.shape)
    mask_new = mask_new.reshape(kv_local, rows_count, steps_count * query_group, steps_count)
    new_scores = jnp.where(
        mask_new,
        new_scores.reshape(kv_local, rows_count, steps_count * query_group, steps_count),
        lowest,
    )
    peak = jnp.maximum(row_max, jnp.max(new_scores, axis=-1))
    slot_peak = jnp.take(peak, row_safe, axis=1)
    weights = jnp.where(
        valid[None, :, None, :], jnp.exp(attention_scores - slot_peak[:, :, :, None]), 0.0
    )
    member_float = member.astype(jnp.float32)
    totals = jnp.einsum(
        "br,kbq->krq", member_float, jnp.sum(weights, axis=-1), precision=lax.Precision.HIGHEST
    )
    slot_output = jnp.einsum(
        "kbqt,kbtd->kbqd",
        weights.astype(jnp.bfloat16),
        paged_value_blocks,
        preferred_element_type=jnp.float32,
    )
    partial_value_sum = jnp.einsum(
        "br,kbqd->krqd", member_float, slot_output, precision=lax.Precision.HIGHEST
    )
    new_weights = jnp.where(mask_new, jnp.exp(new_scores - peak[:, :, :, None]), 0.0)
    totals = totals + jnp.sum(new_weights, axis=-1)
    partial_value_sum = partial_value_sum + jnp.einsum(
        "krqt,trkd->krqd",
        new_weights.astype(jnp.bfloat16),
        step_values,
        preferred_element_type=jnp.float32,
    )
    partial_value_sum = partial_value_sum.reshape(
        kv_local, rows_count, steps_count, query_group, head_size
    ).transpose(2, 1, 0, 3, 4)
    partial_value_sum = partial_value_sum.reshape(
        steps_count * rows_count, kv_local * query_group, head_size
    )
    peak = peak.reshape(kv_local, rows_count, steps_count, query_group).transpose(2, 1, 0, 3)
    peak = peak.reshape(steps_count * rows_count, kv_local * query_group)
    totals = totals.reshape(kv_local, rows_count, steps_count, query_group).transpose(2, 1, 0, 3)
    totals = totals.reshape(steps_count * rows_count, kv_local * query_group)
    moved, peaks, sums = (
        lax.all_to_all(partial_value_sum, "head", split_axis=0, concat_axis=1, tiled=True),
        lax.all_to_all(peak, "head", split_axis=0, concat_axis=1, tiled=True),
        lax.all_to_all(totals, "head", split_axis=0, concat_axis=1, tiled=True),
    )
    stacked = (
        lax.all_to_all(moved[None], "kv", split_axis=2, concat_axis=0, tiled=True),
        lax.all_to_all(peaks[None], "kv", split_axis=2, concat_axis=0, tiled=True),
        lax.all_to_all(sums[None], "kv", split_axis=2, concat_axis=0, tiled=True),
    )
    highest = jnp.max(stacked[1], axis=0)
    rescale = jnp.exp(stacked[1] - highest[None])
    numer = jnp.sum(stacked[0] * rescale[:, :, :, None], axis=0)
    denom = jnp.sum(stacked[2] * rescale, axis=0)
    return numer / denom[:, :, None]


def solution(mesh):
    in_specs = (
        P("head", "kv", None),
        P("head", "kv", None),
        P("head", "kv", None),
        P(None, None, "head", None),
        P(None, None, "head", None),
        P(),
        P(None, "kv"),
    )
    out_specs = P("head", "kv", None)
    return jax.shard_map(
        on_device, mesh=mesh, in_specs=in_specs, out_specs=out_specs, check_vma=False
    )
```

profile of v0, /device:TPU:1, one launch (start us, length us, event | category | flops | bytes accessed | tf_op | source)
XLA Modules:
  0.0 171.4 jit_solution(4267141474127258645)
XLA Ops:
  6.5 0.8 copy.144
  7.4 26.3 %all_gather.6 = bf16[4,128,128]{2,0,1:T(4,128)(2,1)S(1)} all-gather(bf16[4,4,128]{2,0,1:T(4,128)(2,1)S(1)} %copy.144), channel_id=1, replica_groups=mesh['kv'=32,'head'=8] {'kv'}, dimensions={1}, use_global_device_ids=true | all-gather | bytes 135168 | tf_op jit(solution)/shard_map/all_gather | solution.py:24
  33.7 0.7 copy.145
  34.4 0.1 copy.150
  34.7 0.7 fusion.24
  35.4 1.4 gather_fusion
  36.8 0.7 broadcast_compare_fusion
  37.5 0.8 slice_bitcast_fusion
  38.3 0.7 broadcast_select_fusion.2
  39.1 29.3 %all-gather.2.cloned.1.call-done = bf16[32,128,128]{2,1,0:T(8,128)(2,1)} async-done(((bf16[4,128,128]{2,1,0:T(8,128)(2,1)}), bf16[32,128,128]{2,1,0:T(8,128)(2,1)}) %all-gather.2.cloned.1.call-update) | async-done | bytes 1048592 | tf_op jit(solution)/shard_map/all_gather | solution.py:25
  68.3 0.9 constant_dynamic-slice_fusion
  69.3 1.1 fusion.14
  70.6 1.4 gather_fusion.1
  71.9 1.1 bitcast_select_fusion
  73.1 2.4 %fusion.27 = (f32[48,32]{1,0:T(8,128)S(1)}, f32[48,32,256]{2,1,0:T(8,128)}) fusion(bf16[48,32,128]{2,1,0:T(8,128)(2,1)S(1)} %bitcast.105, bf16[48,256,128]{2,1,0:T(8,128)(2,1)S(1)} %bitcast.101, pred[48,256]{1,0:T(8,128)(4,1)S(1)} %fusion.13), kind=kOutput, calls=%fused_computation.58 | convolution fusion | flops 101841408 | bytes 5130240 | tf_op jit(solution)/shard_map/kbqd,kbtd->kbqt/dot_general | solution.py:39
  75.5 0.2 select_reduce_fusion
  75.9 0.6 gather_fusion.2
  76.6 0.2 select_reduce_fusion.1
  76.8 0.6 copy.158
  77.4 4.6 %all-to-all-start.2 = ((f32[8,4,16]{2,1,0:T(4,128)}), f32[8,4,16]{2,1,0:T(4,128)S(1)}, u32[]{:S(2)}, u32[]{:S(2)}) async-start(f32[8,4,16]{2,1,0:T(4,128)} %bitcast.31), calls=%async_computation.2 | async-start | bytes 32768 | tf_op jit(solution)/shard_map/all_to_all | solution.py:102
  82.0 2.1 %fusion = f32[48,32]{1,0:T(8,128)S(1)} fusion(f32[48,32,256]{2,1,0:T(8,128)} %get-tuple-element.14, f32[48,32]{1,0:T(8,128)S(1)} %broadcast_select_fusion.1, pred[48,256]{1,0:T(8,128)(4,1)S(1)} %fusion.13), kind=kLoop, calls=%fused_computation.5 | loop fusion | flops 1178112 | bytes 1597440 | tf_op jit(solution)/shard_map/reduce_sum | solution.py:71
  84.1 3.5 %fusion.4 = f32[48,32,128]{2,1,0:T(8,128)} fusion(bf16[48,256,128]{2,1,0:T(8,128)(2,1)} %bitcast.102, f32[48,32,256]{2,1,0:T(8,128)S(1)} %copy-done.1, f32[48,32]{1,0:T(8,128)S(1)} %broadcast_select_fusion.1, pred[48,256]{1,0:T(8,128)(4,1)S(1)} %fusion.13), kind=kOutput, calls=%fused_computation.12 | convolution fusion | flops 101842944 | bytes 5523456 | tf_op jit(solution)/shard_map/kbqt,kbtd->kbqd/dot_general | solution.py:73
  87.6 0.1 fusion.3
  87.8 0.6 copy.163
  88.4 0.2 all-to-all-done.2
  88.7 6.4 %all-to-all-start.4 = ((f32[8,4,16]{2,1,0:T(4,128)}), f32[8,4,16]{2,1,0:T(4,128)S(1)}, u32[]{:S(2)}, u32[]{:S(2)}) async-start(f32[8,4,16]{2,1,0:T(4,128)} %bitcast.40), calls=%async_computation.4 | async-start | bytes 32768 | tf_op jit(solution)/shard_map/all_to_all | solution.py:103
  95.1 0.2 fusion.18
  95.3 0.7 copy.172
  96.1 5.6 %all-to-all-done.4 = f32[8,4,16]{2,1,0:T(4,128)S(1)} async-done(((f32[8,4,16]{2,1,0:T(4,128)}), f32[8,4,16]{2,1,0:T(4,128)S(1)}, u32[]{:S(2)}, u32[]{:S(2)}) %all-to-all-start.4) | async-done | bytes 2080 | tf_op jit(solution)/shard_map/all_to_all | solution.py:103
  101.7 14.0 %all-to-all-start.3 = ((f32[1,4,128]{1,0,2:T(1,128)}), f32[1,4,128]{1,0,2:T(1,128)S(1)}, u32[]{:S(2)}, u32[]{:S(2)}) async-start(f32[1,4,128]{1,0,2:T(1,128)} %bitcast.33), calls=%async_computation.3 | async-start | bytes 131072 | tf_op jit(solution)/shard_map/all_to_all | solution.py:107
  115.7 2.0 %fusion.2 = f32[1,16,32,128]{3,1,2,0:T(8,128)S(1)} fusion(f32[48,32,128]{2,1,0:T(8,128)} %fusion.4, f32[16,32,128]{2,1,0:T(8,128)S(1)} %fusion.18, s32[48]{0:T(128)S(1)} %get-tuple-element.9), kind=kOutput, calls=%fused_computation.8 | convolution fusion | flops 37815040 | bytes 1310912 | tf_op jit(solution)/shard_map/br,kbqd->krqd/dot_general | solution.py:79
  117.7 0.8 copy.155
  118.4 4.5 %all-to-all-done.3 = f32[1,4,128]{1,0,2:T(1,128)S(1)} async-done(((f32[1,4,128]{1,0,2:T(1,128)}), f32[1,4,128]{1,0,2:T(1,128)S(1)}, u32[]{:S(2)}, u32[]{:S(2)}) %all-to-all-start.3) | async-done | bytes 2080 | tf_op jit(solution)/shard_map/all_to_all | solution.py:107
  123.0 3.4 %all-to-all-start = ((f32[32,16,128]{2,1,0:T(8,128)}), f32[32,16,128]{2,1,0:T(8,128)S(1)}, u32[]{:S(2)}, u32[]{:S(2)}) async-start(f32[32,16,128]{2,1,0:T(8,128)} %bitcast.109), calls=%async_computation | async-start | bytes 524288 | tf_op jit(solution)/shard_map/all_to_all | solution.py:101
  126.4 0.8 copy.174
  127.2 11.5 %all-to-all-done = f32[32,16,128]{2,1,0:T(8,128)S(1)} async-done(((f32[32,16,128]{2,1,0:T(8,128)}), f32[32,16,128]{2,1,0:T(8,128)S(1)}, u32[]{:S(2)}, u32[]{:S(2)}) %all-to-all-start) | async-done | bytes 262176 | tf_op jit(solution)/shard_map/all_to_all | solution.py:101
  138.6 4.6 %all-to-all-start.5 = ((f32[1,4,128]{1,0,2:T(1,128)}), f32[1,4,128]{1,0,2:T(1,128)}, u32[]{:S(2)}, u32[]{:S(2)}) async-start(f32[1,4,128]{1,0,2:T(1,128)} %bitcast.42), calls=%async_computation.5 | async-start | bytes 131072 | tf_op jit(solution)/shard_map/all_to_all | solution.py:108
  143.3 0.3 copy.173
  143.6 0.9 copy.157
  144.5 6.3 %all-to-all-done.5 = f32[1,4,128]{1,0,2:T(1,128)} async-done(((f32[1,4,128]{1,0,2:T(1,128)}), f32[1,4,128]{1,0,2:T(1,128)}, u32[]{:S(2)}, u32[]{:S(2)}) %all-to-all-start.5) | async-done | bytes 2080 | tf_op jit(solution)/shard_map/all_to_all | solution.py:108
  150.8 3.9 %all-to-all-start.1 = ((f32[1,4,128,128]{3,1,0,2:T(4,128)}), f32[1,4,128,128]{3,1,0,2:T(4,128)S(1)}, u32[]{:S(2)}, u32[]{:S(2)}) async-start(f32[1,4,128,128]{3,1,0,2:T(4,128)} %copy.157), calls=%async_computation.1 | async-start | bytes 524288 | tf_op jit(solution)/shard_map/all_to_all | solution.py:106
  154.7 1.8 %copy.175 = f32[1,4,32,4]{3,2,1,0:T(8,128)} copy(f32[1,4,32,4]{1,3,2,0:T(4,128)} %bitcast.43) | data formatting | bytes 4096 | tf_op jit(solution)/shard_map/all_to_all | solution.py:108
  156.5 0.9 fusion.11
  157.4 0.1 copy.167
  157.5 0.3 copy.162
  157.8 5.9 %all-to-all-done.1 = f32[1,4,128,128]{3,1,0,2:T(4,128)S(1)} async-done(((f32[1,4,128,128]{3,1,0,2:T(4,128)}), f32[1,4,128,128]{3,1,0,2:T(4,128)S(1)}, u32[]{:S(2)}, u32[]{:S(2)}) %all-to-all-start.1) | async-done | bytes 262176 | tf_op jit(solution)/shard_map/all_to_all | solution.py:106
  163.7 0.2 multiply_reduce_fusion
  164.0 0.6 copy.168
  (32 shorter events, 1.2 us)
Async XLA Ops:
  6.5 66.5 %copy-start = (bf16[1,12288,128]{2,1,0:T(8,128)(2,1)S(1)}, bf16[1,12288,128]{2,1,0:T(8,128)(2,1)}, u32[]{:S(2)}) copy-start(bf16[1,12288,128]{2,1,0:T(8,128)(2,1)} %param.8) | copy-start | bytes 9437188
  6.5 61.8 %all-gather.2.cloned.1.call-start = ((), (), s32[]{:S(2)}) async-start(), calls=%async_computation.6 | async-start | bytes 1179648 | tf_op jit(solution)/shard_map/all_gather | solution.py:25
  77.4 11.2 %all-to-all-start.2 = ((f32[8,4,16]{2,1,0:T(4,128)}), f32[8,4,16]{2,1,0:T(4,128)S(1)}, u32[]{:S(2)}, u32[]{:S(2)}) async-start(f32[8,4,16]{2,1,0:T(4,128)} %bitcast.31), calls=%async_computation.2 | async-start | bytes 32768 | tf_op jit(solution)/shard_map/all_to_all | solution.py:102
  82.0 2.1 %copy-start.1 = (f32[48,32,256]{2,1,0:T(8,128)S(1)}, f32[48,32,256]{2,1,0:T(8,128)}, u32[]{:S(2)}) copy-start(f32[48,32,256]{2,1,0:T(8,128)} %get-tuple-element.14) | copy-start | bytes 4718596
  84.1 11.0 %copy-start.2 = (bf16[2,16,1,128]{3,1,2,0:T(8,128)(2,1)S(1)}, bf16[2,16,1,128]{3,1,2,0:T(8,128)(2,1)}, u32[]{:S(2)}) copy-start(bf16[2,16,1,128]{3,1,2,0:T(8,128)(2,1)} %param.11) | copy-start | bytes 24580
  88.7 13.0 %all-to-all-start.4 = ((f32[8,4,16]{2,1,0:T(4,128)}), f32[8,4,16]{2,1,0:T(4,128)S(1)}, u32[]{:S(2)}, u32[]{:S(2)}) async-start(f32[8,4,16]{2,1,0:T(4,128)} %bitcast.40), calls=%async_computation.4 | async-start | bytes 32768 | tf_op jit(solution)/shard_map/all_to_all | solution.py:103
  101.7 21.3 %all-to-all-start.3 = ((f32[1,4,128]{1,0,2:T(1,128)}), f32[1,4,128]{1,0,2:T(1,128)S(1)}, u32[]{:S(2)}, u32[]{:S(2)}) async-start(f32[1,4,128]{1,0,2:T(1,128)} %bitcast.33), calls=%async_computation.3 | async-start | bytes 131072 | tf_op jit(solution)/shard_map/all_to_all | solution.py:107
  123.0 15.7 %all-to-all-start = ((f32[32,16,128]{2,1,0:T(8,128)}), f32[32,16,128]{2,1,0:T(8,128)S(1)}, u32[]{:S(2)}, u32[]{:S(2)}) async-start(f32[32,16,128]{2,1,0:T(8,128)} %bitcast.109), calls=%async_computation | async-start | bytes 524288 | tf_op jit(solution)/shard_map/all_to_all | solution.py:101
  138.6 12.1 %all-to-all-start.5 = ((f32[1,4,128]{1,0,2:T(1,128)}), f32[1,4,128]{1,0,2:T(1,128)}, u32[]{:S(2)}, u32[]{:S(2)}) async-start(f32[1,4,128]{1,0,2:T(1,128)} %bitcast.42), calls=%async_computation.5 | async-start | bytes 131072 | tf_op jit(solution)/shard_map/all_to_all | solution.py:108
  150.8 12.9 %all-to-all-start.1 = ((f32[1,4,128,128]{3,1,0,2:T(4,128)}), f32[1,4,128,128]{3,1,0,2:T(4,128)S(1)}, u32[]{:S(2)}, u32[]{:S(2)}) async-start(f32[1,4,128,128]{3,1,0,2:T(4,128)} %copy.157), calls=%async_computation.1 | async-start | bytes 524288 | tf_op jit(solution)/shard_map/all_to_all | solution.py:106
Sparse Core Ops, SparseCore 0:
  34.5 33.7 all-gather.1
where the time goes:
time: 172 us; the launch traced here: 171 us
  waiting for transfers between devices  63.4 us (37%)
  starting transfers between devices  36.9 us (21%)
  blocking collectives  26.3 us (15%)
  local copies, waits for them, and re-layouts  14.2 us (8%)
  between operations  13.6 us (8%)
  matrix products  9.32 us (5%)
  other arithmetic  7.71 us (4%)
    all_gather x1, waiting for transfers between devices, on_device(): every = lax.all_gather(wide, 'head', axis=0, tiled=True)  29.3 us
    all_gather x1, blocking collectives, on_device(): wide = lax.all_gather(queries, 'kv', axis=1, tiled=True)  26.3 us
    all_to_all x1, starting transfers between devices, on_device(): lax.all_to_all(peaks[None], 'kv', split_axis=2, concat_axis=0, tiled=True)  14 us
    all_to_all x1, waiting for transfers between devices, on_device(): lax.all_to_all(partial_value_sum, 'head', split_axis=0, concat_axis=1, ti...  11.5 us
    all_to_all x1, starting transfers between devices, on_device(): lax.all_to_all(totals, 'head', split_axis=0, concat_axis=1, tiled=True)  6.42 us
    all_to_all x1, waiting for transfers between devices, on_device(): lax.all_to_all(sums[None], 'kv', split_axis=2, concat_axis=0, tiled=True)  6.26 us
    all_to_all x1, waiting for transfers between devices, on_device(): lax.all_to_all(moved[None], 'kv', split_axis=2, concat_axis=0, tiled=True)  5.92 us
    all_to_all x1, waiting for transfers between devices, on_device(): lax.all_to_all(totals, 'head', split_axis=0, concat_axis=1, tiled=True)  5.64 us
  transfers between devices with their start and end apart: 7, of which 7 were waited for; matrix products, arithmetic and copies ran while one was open for 12% of the time, Pallas kernels for 0%

commit v1 on v0

v1 whole, which is shorter than its diff:
```python
import functools
import math

import jax
import jax.numpy as jnp
from jax import lax
from jax.experimental import pallas as pl
from jax.experimental.pallas import tpu as pltpu
from jax.sharding import PartitionSpec as P

STEPS = 2
ROWS = 16
GROUP = 16
HEAD = 128
BLOCK = 256
LOCAL_BLOCKS = 48
SHARDS = 32
QUERIES = STEPS * GROUP
EMPTY = -1e20
MASKED = -1e30
SCALE = math.log2(math.e) / math.sqrt(HEAD)
CHUNK = 24


def pieces():
    for r in range(ROWS):
        for s in range(STEPS):
            for b in range(4):
                yield r * QUERIES + s * GROUP + b * 4, (s * 4 + r // 4) * 4 + b, (r % 4) * 4


def attend(table, lengths, q_ref, k_ref, v_ref, sk_ref, sv_ref, out_ref, wide, qs, scores, peak, total, acc):
    wide[...] = q_ref[...].astype(jnp.float32)
    for at, chunk, inside in pieces():
        acc[pl.ds(at, 4), :] = wide[pl.ds(chunk * 16 + inside, 4), :]
    qs[...] = acc[...].astype(jnp.bfloat16)
    peak[...] = jnp.full_like(peak, EMPTY)
    total[...] = jnp.zeros_like(total)
    acc[...] = jnp.zeros_like(acc)

    lane = lax.broadcasted_iota(jnp.int32, (QUERIES, BLOCK), 1)

    def rows_of(b):
        row = table[0, b]
        r = jnp.maximum(row, 0)
        live = jnp.where(row >= 0, lengths[r] - table[1, b] * BLOCK, 0)
        return pl.ds(pl.multiple_of(r * QUERIES, QUERIES), QUERIES), live

    me = lax.axis_index("kv")
    mine = jnp.minimum(me, ROWS - 1)
    mine_rows = pl.ds(pl.multiple_of(mine * QUERIES, QUERIES), QUERIES)
    column = lax.broadcasted_iota(jnp.int32, (QUERIES, QUERIES), 1)
    query = lax.broadcasted_iota(jnp.int32, (QUERIES, QUERIES), 0)
    seen = ((column == mine) | ((column == mine + ROWS) & (query >= GROUP))) & (me < ROWS)
    new = lax.dot_general(
        qs[mine_rows, :], sk_ref[...], (((1,), (1,)), ((), ())), preferred_element_type=jnp.float32
    )
    new = jnp.where(seen, new * SCALE, MASKED)
    peak[mine_rows, :] = jnp.maximum(
        peak[mine_rows, :], jnp.broadcast_to(jnp.max(new, axis=1, keepdims=True), (QUERIES, HEAD))
    )

    for b in range(LOCAL_BLOCKS):
        rows, live = rows_of(b)
        s = lax.dot_general(
            qs[rows, :],
            k_ref[pl.ds(b * BLOCK, BLOCK), :],
            (((1,), (1,)), ((), ())),
            preferred_element_type=jnp.float32,
        )
        s = jnp.where(lane < live, s * SCALE, MASKED)
        scores[b] = s
        peak[rows, :] = jnp.maximum(peak[rows, :], jnp.maximum(s[:, :HEAD], s[:, HEAD:]))

    for r in range(ROWS):
        at = pl.ds(r * QUERIES, QUERIES)
        top = jnp.max(peak[at, :], axis=1, keepdims=True)
        peak[at, :] = jnp.broadcast_to(top, (QUERIES, HEAD))

    p = jnp.exp2(new - peak[mine_rows, :][:, :QUERIES])
    acc[mine_rows, :] = jnp.dot(
        p.astype(jnp.bfloat16), sv_ref[...], preferred_element_type=jnp.float32
    )
    first = lax.broadcasted_iota(jnp.int32, (QUERIES, HEAD), 1) == 0
    total[mine_rows, :] = jnp.where(first, jnp.sum(p, axis=1, keepdims=True), 0.0)

    for b in range(LOCAL_BLOCKS):
        rows, _ = rows_of(b)
        top = peak[rows, :]
        s = scores[b]
        left = jnp.exp2(s[:, :HEAD] - top)
        right = jnp.exp2(s[:, HEAD:] - top)
        p = jnp.concatenate([left.astype(jnp.bfloat16), right.astype(jnp.bfloat16)], axis=1)
        total[rows, :] += left + right
        acc[rows, :] += jnp.dot(
            p, v_ref[pl.ds(b * BLOCK, BLOCK), :], preferred_element_type=jnp.float32
        )

    place = lax.broadcasted_iota(jnp.int32, (QUERIES, HEAD), 1)
    for r in range(ROWS):
        if r % 4 < 2:
            at, after = pl.ds(r * QUERIES, QUERIES), pl.ds((r + 2) * QUERIES, QUERIES)
            one = jnp.sum(total[at, :], axis=1, keepdims=True)
            two = jnp.sum(total[after, :], axis=1, keepdims=True)
            total[at, :] = jnp.where(
                place < 2,
                jnp.where(place == 0, peak[at, :], one),
                jnp.where(place == 2, peak[after, :], two),
            )
    for at, chunk, inside in pieces():
        out_ref[pl.ds(chunk * CHUNK + inside, 4), :] = acc[pl.ds(at, 4), :]
        if inside < 8:
            out_ref[pl.ds(chunk * CHUNK + 16 + inside, 4), :] = total[pl.ds(at, 4), :]


def combine(in_ref, out_ref):
    for half in range(2):
        sides = [in_ref[j, pl.ds(16, 8), :] for j in range(SHARDS)]
        maxima = [side[:, 2 * half : 2 * half + 1] for side in sides]
        top = functools.reduce(jnp.maximum, maxima)
        numer = jnp.zeros((8, HEAD), jnp.float32)
        denom = jnp.zeros((8, 1), jnp.float32)
        for j in range(SHARDS):
            w = jnp.exp2(maxima[j] - top)
            numer += w * in_ref[j, pl.ds(8 * half, 8), :]
            denom += w * sides[j][:, 2 * half + 1 : 2 * half + 2]
        out_ref[pl.ds(8 * half, 8), :] = numer / denom


def on_device(queries, keys, values, step_keys, step_values, lengths, block_table):
    axes = ("kv", "head")
    swap = [
        ((4 * a + b) * 8 + h, (4 * h + b) * 8 + a) for a in range(8) for b in range(4) for h in range(8)
    ]
    q = lax.ppermute(queries.reshape(16, HEAD), axes, swap)
    q = lax.all_to_all(
        jnp.broadcast_to(q[None], (SHARDS, 16, HEAD)), "kv", split_axis=0, concat_axis=0, tiled=True
    )
    vmem = pl.BlockSpec(memory_space=pltpu.VMEM)
    smem = pl.BlockSpec(memory_space=pltpu.SMEM)
    partial = pl.pallas_call(
        attend,
        out_shape=jax.ShapeDtypeStruct((SHARDS * CHUNK, HEAD), jnp.float32),
        in_specs=[smem, smem] + [vmem] * 5,
        out_specs=vmem,
        scratch_shapes=[
            pltpu.VMEM((SHARDS * 16, HEAD), jnp.float32),
            pltpu.VMEM((ROWS * QUERIES, HEAD), jnp.bfloat16),
            pltpu.VMEM((LOCAL_BLOCKS, QUERIES, BLOCK), jnp.float32),
            pltpu.VMEM((ROWS * QUERIES, HEAD), jnp.float32),
            pltpu.VMEM((ROWS * QUERIES, HEAD), jnp.float32),
            pltpu.VMEM((ROWS * QUERIES, HEAD), jnp.float32),
        ],
        compiler_params=pltpu.CompilerParams(vmem_limit_bytes=32 * 1024 * 1024),
        name="attend",
    )(
        block_table,
        lengths,
        q.reshape(SHARDS * 16, HEAD),
        keys.reshape(LOCAL_BLOCKS * BLOCK, HEAD),
        values.reshape(LOCAL_BLOCKS * BLOCK, HEAD),
        step_keys.reshape(STEPS * ROWS, HEAD),
        step_values.reshape(STEPS * ROWS, HEAD),
    )
    moved = lax.all_to_all(
        partial.reshape(SHARDS, CHUNK, HEAD), "kv", split_axis=0, concat_axis=0, tiled=True
    )
    mine = pl.pallas_call(
        combine,
        out_shape=jax.ShapeDtypeStruct((16, HEAD), jnp.float32),
        in_specs=[vmem],
        out_specs=vmem,
        name="combine",
    )(moved)
    return lax.ppermute(mine, axes, swap).reshape(4, 4, HEAD)


def solution(mesh):
    in_specs = (
        P("head", "kv", None),
        P("head", "kv", None),
        P("head", "kv", None),
        P(None, None, "head", None),
        P(None, None, "head", None),
        P(),
        P(None, "kv"),
    )
    out_specs = P("head", "kv", None)
    return jax.shard_map(
        on_device, mesh=mesh, in_specs=in_specs, out_specs=out_specs, check_vma=False
    )
```

time: 172 us -> 64.2 us (0.37)
  the two profiles are of different devices: /device:TPU:1 before, /device:TPU:199 now
where the time goes in v1:
time: 64.2 us; the launch traced here: 63.7 us
  blocking collectives  27.8 us (43%)
  waiting for transfers between devices  17.6 us (27%)
  local copies, waits for them, and re-layouts  7.12 us (11%)
  starting transfers between devices  6.96 us (11%)
  Pallas kernels  4.24 us (7%)
    all_to_all x1, blocking collectives, on_device(): lax.all_to_all(partial.reshape(SHARDS, CHUNK, HEAD), 'kv', split_axis=0,...  14.3 us
    all_to_all x1, blocking collectives, on_device(): lax.all_to_all(jnp.broadcast_to(q[None], (SHARDS, 16, HEAD)), 'kv', split...  13.5 us
    ppermute x1, waiting for transfers between devices, on_device(): return lax.ppermute(mine, axes, swap).reshape(4, 4, HEAD)  9.59 us
    ppermute x1, waiting for transfers between devices, on_device(): q = lax.ppermute(queries.reshape(16, HEAD), axes, swap)  7.97 us
    unnamed x13, local copies, waits for them, and re-layouts  7.1 us
    ppermute x1, starting transfers between devices, on_device(): q = lax.ppermute(queries.reshape(16, HEAD), axes, swap)  4.1 us
    ppermute x1, starting transfers between devices, on_device(): return lax.ppermute(mine, axes, swap).reshape(4, 4, HEAD)  2.87 us
    pallas_call x1, Pallas kernels, on_device(): pl.pallas_call(attend, out_shape=jax.ShapeDtypeStruct((SHARDS * CHUNK, HE...  2.37 us
  transfers between devices with their start and end apart: 2, of which 2 were waited for; matrix products, arithmetic and copies ran while one was open for 0% of the time, Pallas kernels for 0%

profile of v1, /device:TPU:199, one launch (start us, length us, event | category | flops | bytes accessed | tf_op | source)
XLA Modules:
  0.0 63.7 jit_solution(3510424384954226168)
XLA Ops:
  0.0 4.1 %collective-permute-start = (bf16[16,128]{1,0:T(8,128)(2,1)}, bf16[16,128]{1,0:T(8,128)(2,1)S(1)}, u32[]{:S(2)}, u32[]{:S(2)}) collective-permute-start(bf16[16,128]{1,0:T(8,128)(2,1)} %bitcast.15), channel_id=1, source_target_pairs={{0,0},{1,32},{2,64},{3,96},{4,128},{5,160},{6,192},{7,224},{8,8},{... | collective-permute-start | bytes 12296 | tf_op jit(solution)/shard_map/ppermute | solution.py:135
  4.1 8.0 %collective-permute-done = bf16[16,128]{1,0:T(8,128)(2,1)S(1)} collective-permute-done((bf16[16,128]{1,0:T(8,128)(2,1)}, bf16[16,128]{1,0:T(8,128)(2,1)S(1)}, u32[]{:S(2)}, u32[]{:S(2)}) %collective-permute-start) | collective-permute-done | bytes 4128 | tf_op jit(solution)/shard_map/ppermute | solution.py:135
  12.1 13.5 %all_to_all.10 = bf16[32,16,128]{2,1,0:T(8,128)(2,1)S(1)} all-to-all(bf16[32,16,128]{2,1,0:T(8,128)(2,1)S(1)} %broadcast_in_dim.2), channel_id=1, replica_groups=mesh['kv'=32,'head'=8] {'kv'}, dimensions={0} | all-to-all | bytes 262144 | tf_op jit(solution)/shard_map/all_to_all | solution.py:136
  25.6 0.0 copy-start
  25.6 1.9 %copy-done = bf16[1,12288,128]{2,1,0:T(8,128)(2,1)S(1)} copy-done((bf16[1,12288,128]{2,1,0:T(8,128)(2,1)S(1)}, bf16[1,12288,128]{2,1,0:T(8,128)(2,1)}, u32[]{:S(2)}) %copy-start) | copy-done | bytes 3145752
  27.5 0.0 copy-start.1
  27.5 1.9 %copy-done.1 = bf16[1,12288,128]{2,1,0:T(8,128)(2,1)S(1)} copy-done((bf16[1,12288,128]{2,1,0:T(8,128)(2,1)S(1)}, bf16[1,12288,128]{2,1,0:T(8,128)(2,1)}, u32[]{:S(2)}) %copy-start.1) | copy-done | bytes 3145752
  29.4 0.0 copy-start.2
  29.4 0.7 %copy-done.2 = bf16[2,16,1,128]{3,1,2,0:T(8,128)(2,1)S(1)} copy-done((bf16[2,16,1,128]{3,1,2,0:T(8,128)(2,1)S(1)}, bf16[2,16,1,128]{3,1,2,0:T(8,128)(2,1)}, u32[]{:S(2)}) %copy-start.2) | copy-done | bytes 8216
  30.1 0.0 copy-start.3
  30.1 0.7 %copy-done.3 = bf16[2,16,1,128]{3,1,2,0:T(8,128)(2,1)S(1)} copy-done((bf16[2,16,1,128]{3,1,2,0:T(8,128)(2,1)S(1)}, bf16[2,16,1,128]{3,1,2,0:T(8,128)(2,1)}, u32[]{:S(2)}) %copy-start.3) | copy-done | bytes 8216
  30.8 0.0 copy-start.4
  30.8 0.7 %copy-done.4 = s32[2,48]{1,0:T(2,128)S(1)} copy-done((s32[2,48]{1,0:T(2,128)S(1)}, s32[2,48]{1,0:T(2,128)}, u32[]{:S(2)}) %copy-start.4) | copy-done | bytes 408
  31.5 0.0 copy-start.5
  31.5 0.7 %copy-done.5 = s32[16]{0:T(128)S(1)} copy-done((s32[16]{0:T(128)S(1)}, s32[16]{0:T(128)}, u32[]{:S(2)}) %copy-start.5) | copy-done | bytes 88
  32.1 2.4 %attend.1 = f32[768,128]{1,0:T(8,128)S(1)} custom-call(s32[2,48]{1,0:T(2,128)S(1)} %copy-done.4, s32[16]{0:T(128)S(1)} %copy-done.5, bf16[512,128]{1,0:T(8,128)(2,1)S(1)} %bitcast.11, bf16[12288,128]{1,0:T(8,128)(2,1)S(1)} %bitcast.8, bf16[12288,128]{1,0:T(8,128)(2,1)S(1)} %bitcast.9, bf16[32,128]{1,0:T(8,128)(2,1)S(1)} %bitcast.12, bf16[32,128]{1,0:T(8,128)(2,1)S(1)} %bitcast.13), custom_call_target="tpu_custom_call" | custom-call | tf_op jit(solution)/shard_map/attend/pallas_call | solution.py:141
  34.5 14.3 %all_to_all.11.in_ref = f32[32,24,128]{2,1,0:T(8,128)} all-to-all(f32[32,24,128]{2,1,0:T(8,128)S(1)} %bitcast.10), channel_id=1, replica_groups=mesh['kv'=32,'head'=8] {'kv'}, dimensions={0} | all-to-all | bytes 786432 | tf_op jit(solution)/shard_map/all_to_all | solution.py:165
  48.8 1.9 %combine.1 = f32[16,128]{1,0:T(8,128)} custom-call(f32[32,24,128]{2,1,0:T(8,128)} %all_to_all.11.in_ref), custom_call_target="tpu_custom_call" | custom-call | tf_op jit(solution)/shard_map/combine/pallas_call | solution.py:168
  50.7 2.9 %collective-permute-start.1 = (f32[16,128]{1,0:T(8,128)}, f32[16,128]{1,0:T(8,128)S(1)}, u32[]{:S(2)}, u32[]{:S(2)}) collective-permute-start(f32[16,128]{1,0:T(8,128)} %combine.1), channel_id=1, source_target_pairs={{0,0},{1,32},{2,64},{3,96},{4,128},{5,160},{6,192},{7,224},{8,8},{... | collective-permute-start | bytes 24584 | tf_op jit(solution)/shard_map/ppermute | solution.py:175
  53.5 9.6 %collective-permute-done.1 = f32[16,128]{1,0:T(8,128)S(1)} collective-permute-done((f32[16,128]{1,0:T(8,128)}, f32[16,128]{1,0:T(8,128)S(1)}, u32[]{:S(2)}, u32[]{:S(2)}) %collective-permute-start.1) | collective-permute-done | bytes 8224 | tf_op jit(solution)/shard_map/ppermute | solution.py:175
  63.1 0.6 copy.9
  (1 shorter events, 0.0 us)
Async XLA Ops:
  0.0 12.1 %collective-permute-start = (bf16[16,128]{1,0:T(8,128)(2,1)}, bf16[16,128]{1,0:T(8,128)(2,1)S(1)}, u32[]{:S(2)}, u32[]{:S(2)}) collective-permute-start(bf16[16,128]{1,0:T(8,128)(2,1)} %bitcast.15), channel_id=1, source_target_pairs={{0,0},{1,32},{2,64},{3,96},{4,128},{5,160},{6,192},{7,224},{8,8},{... | collective-permute-start | bytes 12296 | tf_op jit(solution)/shard_map/ppermute | solution.py:135
  25.6 1.9 %copy-start = (bf16[1,12288,128]{2,1,0:T(8,128)(2,1)S(1)}, bf16[1,12288,128]{2,1,0:T(8,128)(2,1)}, u32[]{:S(2)}) copy-start(bf16[1,12288,128]{2,1,0:T(8,128)(2,1)} %param.8) | copy-start | bytes 9437188
  27.5 1.9 %copy-start.1 = (bf16[1,12288,128]{2,1,0:T(8,128)(2,1)S(1)}, bf16[1,12288,128]{2,1,0:T(8,128)(2,1)}, u32[]{:S(2)}) copy-start(bf16[1,12288,128]{2,1,0:T(8,128)(2,1)} %param.9) | copy-start | bytes 9437188
  29.4 0.7 %copy-start.2 = (bf16[2,16,1,128]{3,1,2,0:T(8,128)(2,1)S(1)}, bf16[2,16,1,128]{3,1,2,0:T(8,128)(2,1)}, u32[]{:S(2)}) copy-start(bf16[2,16,1,128]{3,1,2,0:T(8,128)(2,1)} %param.10) | copy-start | bytes 24580
  30.1 0.7 %copy-start.3 = (bf16[2,16,1,128]{3,1,2,0:T(8,128)(2,1)S(1)}, bf16[2,16,1,128]{3,1,2,0:T(8,128)(2,1)}, u32[]{:S(2)}) copy-start(bf16[2,16,1,128]{3,1,2,0:T(8,128)(2,1)} %param.11) | copy-start | bytes 24580
  30.8 0.7 %copy-start.4 = (s32[2,48]{1,0:T(2,128)S(1)}, s32[2,48]{1,0:T(2,128)}, u32[]{:S(2)}) copy-start(s32[2,48]{1,0:T(2,128)} %table.1) | copy-start | bytes 1156
  31.5 0.7 %copy-start.5 = (s32[16]{0:T(128)S(1)}, s32[16]{0:T(128)}, u32[]{:S(2)}) copy-start(s32[16]{0:T(128)} %lengths.1) | copy-start | bytes 196
  50.7 12.5 %collective-permute-start.1 = (f32[16,128]{1,0:T(8,128)}, f32[16,128]{1,0:T(8,128)S(1)}, u32[]{:S(2)}, u32[]{:S(2)}) collective-permute-start(f32[16,128]{1,0:T(8,128)} %combine.1), channel_id=1, source_target_pairs={{0,0},{1,32},{2,64},{3,96},{4,128},{5,160},{6,192},{7,224},{8,8},{... | collective-permute-start | bytes 24584 | tf_op jit(solution)/shard_map/ppermute | solution.py:175

commit v2 on v1

--- a/solution.py
+++ b/solution.py
@@ -20,19 +20,79 @@
 MASKED = -1e30
 SCALE = math.log2(math.e) / math.sqrt(HEAD)
 CHUNK = 24
-
-
-def pieces():
+PARTS = 4
+EARLY = 36
+GRANT = 16 * 1024 * 1024
+
+
+SIDEWAYS = (1, 1, 1, 0, 0, 0, 0, 1)
+UPWARDS = (2, 1, 0, 1, 0, 3, 2, 3)
+
+
+def station(c, h, b):
+    step = (h - c) % 8
+    right = b >> 1
+    x = (2 * (c & 1) + right + (2 * right - 1) * SIDEWAYS[step]) % 4
+    y = ((c >> 1) + UPWARDS[step]) % 4
+    return y * 8 + x * 2 + (b & 1)
+
+
+def stations():
+    sideways = sum(v << i for i, v in enumerate(SIDEWAYS))
+    upwards = sum(v << (2 * i) for i, v in enumerate(UPWARDS))
+    c = lax.axis_index("head")
+    found = {}
+    for h in range(8):
+        step = (h - c) & 7
+        y = ((c >> 1) + (upwards >> (2 * step))) & 3
+        for right in range(2):
+            x = (2 * (c & 1) + right + (2 * right - 1) * ((sideways >> step) & 1)) & 3
+            for core in range(2):
+                found[h, 2 * right + core] = y * 8 + x * 2 + core
+    return found
+
+
+def pieces(found):
     for r in range(ROWS):
         for s in range(STEPS):
             for b in range(4):
-                yield r * QUERIES + s * GROUP + b * 4, (s * 4 + r // 4) * 4 + b, (r % 4) * 4
-
-
-def attend(table, lengths, q_ref, k_ref, v_ref, sk_ref, sv_ref, out_ref, wide, qs, scores, peak, total, acc):
+                yield r * QUERIES + s * GROUP + b * 4, found[s * 4 + r // 4, b], (r % 4) * 4
+
+
+def fetch(*refs):
+    count = len(refs) // 2
+    copies = [
+        pltpu.make_async_copy(refs[i].at[pl.ds(0, refs[count + i].shape[0])], refs[count + i], refs[-1].at[i])
+        for i in range(count)
+    ]
+    for copy in copies:
+        copy.start()
+    for copy in copies:
+        copy.wait()
+
+
+def attend(
+    table_vmem, lengths_vmem, q_ref, early_ref, k_hbm, v_hbm, sk_ref, sv_ref, out_ref,
+    table, lengths, late_ref, v_ref, wide, qs, scores, peak, total, acc, small_sems, k_sem, v_sems,
+):
+    small = [
+        pltpu.make_async_copy(table_vmem, table, small_sems.at[0]),
+        pltpu.make_async_copy(lengths_vmem, lengths, small_sems.at[1]),
+    ]
+    late = pltpu.make_async_copy(
+        k_hbm.at[pl.ds(EARLY * BLOCK, (LOCAL_BLOCKS - EARLY) * BLOCK)], late_ref, k_sem
+    )
+    size = LOCAL_BLOCKS * BLOCK // PARTS
+    v_parts = [
+        pltpu.make_async_copy(v_hbm.at[pl.ds(i * size, size)], v_ref.at[pl.ds(i * size, size)], v_sems.at[i])
+        for i in range(PARTS)
+    ]
+    for copy in small + [late] + v_parts:
+        copy.start()
+    found = stations()
     wide[...] = q_ref[...].astype(jnp.float32)
-    for at, chunk, inside in pieces():
-        acc[pl.ds(at, 4), :] = wide[pl.ds(chunk * 16 + inside, 4), :]
+    for at, chunk, inside in pieces(found):
+        acc[pl.ds(at, 4), :] = wide[chunk, pl.ds(inside, 4), :]
     qs[...] = acc[...].astype(jnp.bfloat16)
     peak[...] = jnp.full_like(peak, EMPTY)
     total[...] = jnp.zeros_like(total)
@@ -46,6 +106,8 @@
         live = jnp.where(row >= 0, lengths[r] - table[1, b] * BLOCK, 0)
         return pl.ds(pl.multiple_of(r * QUERIES, QUERIES), QUERIES), live
 
+    for copy in small:
+        copy.wait()
     me = lax.axis_index("kv")
     mine = jnp.minimum(me, ROWS - 1)
     mine_rows = pl.ds(pl.multiple_of(mine * QUERIES, QUERIES), QUERIES)
@@ -61,10 +123,14 @@
     )
 
     for b in range(LOCAL_BLOCKS):
+        if b == EARLY:
+            late.wait()
         rows, live = rows_of(b)
         s = lax.dot_general(
             qs[rows, :],
-            k_ref[pl.ds(b * BLOCK, BLOCK), :],
+            early_ref[pl.ds(b * BLOCK, BLOCK), :]
+            if b < EARLY
+            else late_ref[pl.ds((b - EARLY) * BLOCK, BLOCK), :],
             (((1,), (1,)), ((), ())),
             preferred_element_type=jnp.float32,
         )
@@ -85,6 +151,8 @@
     total[mine_rows, :] = jnp.where(first, jnp.sum(p, axis=1, keepdims=True), 0.0)
 
     for b in range(LOCAL_BLOCKS):
+        if b % (LOCAL_BLOCKS // PARTS) == 0:
+            v_parts[b // (LOCAL_BLOCKS // PARTS)].wait()
         rows, _ = rows_of(b)
         top = peak[rows, :]
         s = scores[b]
@@ -107,10 +175,10 @@
                 jnp.where(place == 0, peak[at, :], one),
                 jnp.where(place == 2, peak[after, :], two),
             )
-    for at, chunk, inside in pieces():
-        out_ref[pl.ds(chunk * CHUNK + inside, 4), :] = acc[pl.ds(at, 4), :]
+    for at, chunk, inside in pieces(found):
+        out_ref[chunk, pl.ds(inside, 4), :] = acc[pl.ds(at, 4), :]
         if inside < 8:
-            out_ref[pl.ds(chunk * CHUNK + 16 + inside, 4), :] = total[pl.ds(at, 4), :]
+            out_ref[chunk, pl.ds(16 + inside, 4), :] = total[pl.ds(at, 4), :]
 
 
 def combine(in_ref, out_ref):
@@ -124,55 +192,75 @@
             w = jnp.exp2(maxima[j] - top)
             numer += w * in_ref[j, pl.ds(8 * half, 8), :]
             denom += w * sides[j][:, 2 * half + 1 : 2 * half + 2]
-        out_ref[pl.ds(8 * half, 8), :] = numer / denom
+        out_ref[pl.ds(2 * half, 2)] = (numer / denom).reshape(2, 4, HEAD)
 
 
 def on_device(queries, keys, values, step_keys, step_values, lengths, block_table):
     axes = ("kv", "head")
-    swap = [
-        ((4 * a + b) * 8 + h, (4 * h + b) * 8 + a) for a in range(8) for b in range(4) for h in range(8)
-    ]
-    q = lax.ppermute(queries.reshape(16, HEAD), axes, swap)
+    gather = [
+        ((4 * c + b) * 8 + h, station(c, h, b) * 8 + c) for c in range(8) for b in range(4) for h in range(8)
+    ]
+    vmem = pl.BlockSpec(memory_space=pltpu.VMEM)
+    hbm = pl.BlockSpec(memory_space=pltpu.HBM)
+    q = lax.ppermute(queries.reshape(16, HEAD), axes, gather)
+    all_keys = pltpu.with_memory_space_constraint(keys.reshape(LOCAL_BLOCKS * BLOCK, HEAD), pltpu.HBM)
+    all_values = pltpu.with_memory_space_constraint(values.reshape(LOCAL_BLOCKS * BLOCK, HEAD), pltpu.HBM)
+    sources = [
+        keys.reshape(LOCAL_BLOCKS * BLOCK, HEAD),
+        step_keys.reshape(STEPS * ROWS, HEAD),
+        step_values.reshape(STEPS * ROWS, HEAD),
+        block_table,
+        lengths,
+    ]
+    early, new_keys, new_values, table, limits = pl.pallas_call(
+        fetch,
+        out_shape=tuple(
+            jax.ShapeDtypeStruct((EARLY * BLOCK, HEAD) if i == 0 else x.shape, x.dtype)
+            for i, x in enumerate(sources)
+        ),
+        in_specs=[hbm] * 5,
+        out_specs=(vmem,) * 5,
+        scratch_shapes=[pltpu.SemaphoreType.DMA((5,))],
+        compiler_params=pltpu.CompilerParams(vmem_limit_bytes=GRANT),
+        name="fetch",
+    )(*[pltpu.with_memory_space_constraint(x, pltpu.HBM) for x in sources])
+    q, early = lax.optimization_barrier((q, early))
     q = lax.all_to_all(
         jnp.broadcast_to(q[None], (SHARDS, 16, HEAD)), "kv", split_axis=0, concat_axis=0, tiled=True
     )
-    vmem = pl.BlockSpec(memory_space=pltpu.VMEM)
-    smem = pl.BlockSpec(memory_space=pltpu.SMEM)
     partial = pl.pallas_call(
         attend,
-        out_shape=jax.ShapeDtypeStruct((SHARDS * CHUNK, HEAD), jnp.float32),
-        in_specs=[smem, smem] + [vmem] * 5,
+        out_shape=jax.ShapeDtypeStruct((SHARDS, CHUNK, HEAD), jnp.float32),
+        in_specs=[vmem, vmem, vmem, vmem, hbm, hbm, vmem, vmem],
         out_specs=vmem,
         scratch_shapes=[
-            pltpu.VMEM((SHARDS * 16, HEAD), jnp.float32),
+            pltpu.SMEM((2, LOCAL_BLOCKS), jnp.int32),
+            pltpu.SMEM((ROWS,), jnp.int32),
+            pltpu.VMEM(((LOCAL_BLOCKS - EARLY) * BLOCK, HEAD), jnp.bfloat16),
+            pltpu.VMEM((LOCAL_BLOCKS * BLOCK, HEAD), jnp.bfloat16),
+            pltpu.VMEM((SHARDS, 16, HEAD), jnp.float32),
             pltpu.VMEM((ROWS * QUERIES, HEAD), jnp.bfloat16),
             pltpu.VMEM((LOCAL_BLOCKS, QUERIES, BLOCK), jnp.float32),
             pltpu.VMEM((ROWS * QUERIES, HEAD), jnp.float32),
             pltpu.VMEM((ROWS * QUERIES, HEAD), jnp.float32),
             pltpu.VMEM((ROWS * QUERIES, HEAD), jnp.float32),
+            pltpu.SemaphoreType.DMA((2,)),
+            pltpu.SemaphoreType.DMA,
+            pltpu.SemaphoreType.DMA((PARTS,)),
         ],
-        compiler_params=pltpu.CompilerParams(vmem_limit_bytes=32 * 1024 * 1024),
+        compiler_params=pltpu.CompilerParams(vmem_limit_bytes=GRANT),
         name="attend",
-    )(
-        block_table,
-        lengths,
-        q.reshape(SHARDS * 16, HEAD),
-        keys.reshape(LOCAL_BLOCKS * BLOCK, HEAD),
-        values.reshape(LOCAL_BLOCKS * BLOCK, HEAD),
-        step_keys.reshape(STEPS * ROWS, HEAD),
-        step_values.reshape(STEPS * ROWS, HEAD),
-    )
-    moved = lax.all_to_all(
-        partial.reshape(SHARDS, CHUNK, HEAD), "kv", split_axis=0, concat_axis=0, tiled=True
-    )
+    )(table, limits, q, early, all_keys, all_values, new_keys, new_values)
+    moved = lax.all_to_all(partial, "kv", split_axis=0, concat_axis=0, tiled=True)
     mine = pl.pallas_call(
         combine,
-        out_shape=jax.ShapeDtypeStruct((16, HEAD), jnp.float32),
+        out_shape=jax.ShapeDtypeStruct((4, 4, HEAD), jnp.float32),
         in_specs=[vmem],
         out_specs=vmem,
+        compiler_params=pltpu.CompilerParams(vmem_limit_bytes=8 * 1024 * 1024),
         name="combine",
     )(moved)
-    return lax.ppermute(mine, axes, swap).reshape(4, 4, HEAD)
+    return lax.ppermute(mine, axes, [(t, s) for s, t in gather])
 
 
 def solution(mesh):

time: 64.2 us -> 50.1 us (0.78)
  the two profiles are of different devices: /device:TPU:199 before, /device:TPU:224 now
where the time goes in v2:
time: 50.1 us; the launch traced here: 49.9 us
  blocking collectives  27 us (54%)
  waiting for transfers between devices  14.6 us (29%)
  Pallas kernels  5.57 us (11%)
  starting transfers between devices  2.1 us (4%)
  local copies, waits for them, and re-layouts  0.62 us (1%)
    all_to_all x1, blocking collectives, on_device(): lax.all_to_all(partial, 'kv', split_axis=0, concat_axis=0, tiled=True)  13.8 us
    all_to_all x1, blocking collectives, on_device(): lax.all_to_all(jnp.broadcast_to(q[None], (SHARDS, 16, HEAD)), 'kv', split...  13.2 us
    ppermute x1, waiting for transfers between devices, on_device(): return lax.ppermute(mine, axes, [(t, s) for s, t in gather])  9.07 us
    ppermute x1, waiting for transfers between devices, on_device(): q = lax.ppermute(queries.reshape(16, HEAD), axes, gather)  5.5 us
    pallas_call x1, Pallas kernels, on_device(): pl.pallas_call(attend, out_shape=jax.ShapeDtypeStruct((SHARDS, CHUNK, HEA...  3.57 us
    ppermute x1, starting transfers between devices, on_device(): q = lax.ppermute(queries.reshape(16, HEAD), axes, gather)  2.03 us
    pallas_call x1, Pallas kernels, on_device(): pl.pallas_call(fetch, out_shape=tuple((jax.ShapeDtypeStruct((EARLY * BLOC...  1.71 us
  transfers between devices with their start and end apart: 2, of which 2 were waited for; matrix products, arithmetic and copies ran while one was open for 0% of the time, Pallas kernels for 3%

profile of v2, /device:TPU:224, one launch (start us, length us, event | category | flops | bytes accessed | tf_op | source)
XLA Modules:
  0.0 49.9 jit_solution(10544702647481799060)
XLA Ops:
  0.0 2.0 %collective-permute-start = (bf16[16,128]{1,0:T(8,128)(2,1)}, bf16[16,128]{1,0:T(8,128)(2,1)S(1)}, u32[]{:S(2)}, u32[]{:S(2)}) collective-permute-start(bf16[16,128]{1,0:T(8,128)(2,1)} %bitcast.10), channel_id=1, source_target_pairs={{0,176},{1,112},{2,48},{3,64},{4,0},{5,192},{6,128},{7,240},{8,184... | collective-permute-start | bytes 12296 | tf_op jit(solution)/shard_map/ppermute | solution.py:205
  2.0 1.7 %fetch.1 = (bf16[9216,128]{1,0:T(8,128)(2,1)S(1)}, bf16[32,128]{1,0:T(8,128)(2,1)S(1)}, bf16[32,128]{1,0:T(8,128)(2,1)S(1)}, s32[2,48]{1,0:T(2,128)S(1)}, s32[16]{0:T(128)S(1)}) custom-call(bf16[12288,128]{1,0:T(8,128)(2,1)} %bitcast.5, bf16[32,128]{1,0:T(8,128)(2,1)} %bitcast.8, bf16[32,128]{1,0:T(8,128)(2,1)} %bitcast.9, s32[2,48]{1,0:T(2,128)} %refs_3_.1, ...), custom_call_target="tpu_custom_call" | custom-call | tf_op jit(solution)/shard_map/fetch/pallas_call | solution.py:215
  3.7 5.5 %collective-permute-done = bf16[16,128]{1,0:T(8,128)(2,1)S(1)} collective-permute-done((bf16[16,128]{1,0:T(8,128)(2,1)}, bf16[16,128]{1,0:T(8,128)(2,1)S(1)}, u32[]{:S(2)}, u32[]{:S(2)}) %collective-permute-start) | collective-permute-done | bytes 4128 | tf_op jit(solution)/shard_map/ppermute | solution.py:205
  9.3 13.2 %all_to_all.10.q_ref = bf16[32,16,128]{2,1,0:T(8,128)(2,1)S(1)} all-to-all(bf16[32,16,128]{2,1,0:T(8,128)(2,1)S(1)} %broadcast_in_dim.2), channel_id=1, replica_groups=mesh['kv'=32,'head'=8] {'kv'}, dimensions={0} | all-to-all | bytes 262144 | tf_op jit(solution)/shard_map/all_to_all | solution.py:228
  22.5 3.6 %attend.1 = f32[32,24,128]{2,1,0:T(8,128)S(1)} custom-call(s32[2,48]{1,0:T(2,128)S(1)} %get-tuple-element.12.table_vmem, s32[16]{0:T(128)S(1)} %get-tuple-element.13.lengths_vmem, bf16[32,16,128]{2,1,0:T(8,128)(2,1)S(1)} %all_to_all.10.q_ref, bf16[9216,128]{1,0:T(8,128)(2,1)S(1)} %get-tuple-element.16.early_ref, bf16[12288,128]{1,0:T(8,128)(2,1)} %bitcast.6, ...), custom_call_target="tpu_custom_call" | custom-call | tf_op jit(solution)/shard_map/attend/pallas_call | solution.py:231
  26.1 13.8 %all_to_all.11.in_ref = f32[32,24,128]{2,1,0:T(8,128)S(1)} all-to-all(f32[32,24,128]{2,1,0:T(8,128)S(1)} %attend.1), channel_id=1, replica_groups=mesh['kv'=32,'head'=8] {'kv'}, dimensions={0} | all-to-all | bytes 786432 | tf_op jit(solution)/shard_map/all_to_all | solution.py:254
  39.9 0.3 combine.1
  40.1 0.1 collective-permute-start.1
  40.2 9.1 %collective-permute-done.1 = f32[4,4,128]{2,1,0:T(4,128)S(1)} collective-permute-done((f32[4,4,128]{2,1,0:T(4,128)S(1)}, f32[4,4,128]{2,1,0:T(4,128)S(1)}, u32[]{:S(2)}, u32[]{:S(2)}) %collective-permute-start.1) | collective-permute-done | bytes 8224 | tf_op jit(solution)/shard_map/ppermute | solution.py:263
  49.3 0.6 %copy.9 = f32[4,4,128]{2,1,0:T(4,128)} copy(f32[4,4,128]{2,1,0:T(4,128)S(1)} %collective-permute-done.1) | data formatting | bytes 16384
  (1 shorter events, 0.0 us)
Async XLA Ops:
  0.0 9.2 %collective-permute-start = (bf16[16,128]{1,0:T(8,128)(2,1)}, bf16[16,128]{1,0:T(8,128)(2,1)S(1)}, u32[]{:S(2)}, u32[]{:S(2)}) collective-permute-start(bf16[16,128]{1,0:T(8,128)(2,1)} %bitcast.10), channel_id=1, source_target_pairs={{0,176},{1,112},{2,48},{3,64},{4,0},{5,192},{6,128},{7,240},{8,184... | collective-permute-start | bytes 12296 | tf_op jit(solution)/shard_map/ppermute | solution.py:205
  40.1 9.1 %collective-permute-start.1 = (f32[4,4,128]{2,1,0:T(4,128)S(1)}, f32[4,4,128]{2,1,0:T(4,128)S(1)}, u32[]{:S(2)}, u32[]{:S(2)}) collective-permute-start(f32[4,4,128]{2,1,0:T(4,128)S(1)} %combine.1), channel_id=1, source_target_pairs={{176,0},{112,1},{48,2},{64,3},{0,4},{192,5},{128,6},{240,7},{184,8... | collective-permute-start | bytes 24584 | tf_op jit(solution)/shard_map/ppermute | solution.py:263

commit v3 on v2

--- a/solution.py
+++ b/solution.py
@@ -15,13 +15,13 @@
 BLOCK = 256
 LOCAL_BLOCKS = 48
 SHARDS = 32
+CHIPS = 16
 QUERIES = STEPS * GROUP
 EMPTY = -1e20
 MASKED = -1e30
 SCALE = math.log2(math.e) / math.sqrt(HEAD)
 CHUNK = 24
-PARTS = 4
-EARLY = 36
+EARLY = 42
 GRANT = 16 * 1024 * 1024
 
 
@@ -72,8 +72,8 @@
 
 
 def attend(
-    table_vmem, lengths_vmem, q_ref, early_ref, k_hbm, v_hbm, sk_ref, sv_ref, out_ref,
-    table, lengths, late_ref, v_ref, wide, qs, scores, peak, total, acc, small_sems, k_sem, v_sems,
+    table_vmem, lengths_vmem, q_ref, early_ref, k_hbm, v_hbm, sk_ref, sv_ref, keep_ref, send_ref,
+    table, lengths, late_ref, v_ref, wide, qs, scores, peak, total, acc, small_sems, k_sem, v_sem,
 ):
     small = [
         pltpu.make_async_copy(table_vmem, table, small_sems.at[0]),
@@ -82,12 +82,8 @@
     late = pltpu.make_async_copy(
         k_hbm.at[pl.ds(EARLY * BLOCK, (LOCAL_BLOCKS - EARLY) * BLOCK)], late_ref, k_sem
     )
-    size = LOCAL_BLOCKS * BLOCK // PARTS
-    v_parts = [
-        pltpu.make_async_copy(v_hbm.at[pl.ds(i * size, size)], v_ref.at[pl.ds(i * size, size)], v_sems.at[i])
-        for i in range(PARTS)
-    ]
-    for copy in small + [late] + v_parts:
+    fetched = pltpu.make_async_copy(v_hbm, v_ref, v_sem)
+    for copy in small + [late, fetched]:
         copy.start()
     found = stations()
     wide[...] = q_ref[...].astype(jnp.float32)
@@ -106,7 +102,7 @@
         live = jnp.where(row >= 0, lengths[r] - table[1, b] * BLOCK, 0)
         return pl.ds(pl.multiple_of(r * QUERIES, QUERIES), QUERIES), live
 
-    for copy in small:
+    for copy in small + [late]:
         copy.wait()
     me = lax.axis_index("kv")
     mine = jnp.minimum(me, ROWS - 1)
@@ -118,13 +114,7 @@
         qs[mine_rows, :], sk_ref[...], (((1,), (1,)), ((), ())), preferred_element_type=jnp.float32
     )
     new = jnp.where(seen, new * SCALE, MASKED)
-    peak[mine_rows, :] = jnp.maximum(
-        peak[mine_rows, :], jnp.broadcast_to(jnp.max(new, axis=1, keepdims=True), (QUERIES, HEAD))
-    )
-
     for b in range(LOCAL_BLOCKS):
-        if b == EARLY:
-            late.wait()
         rows, live = rows_of(b)
         s = lax.dot_general(
             qs[rows, :],
@@ -138,21 +128,18 @@
         scores[b] = s
         peak[rows, :] = jnp.maximum(peak[rows, :], jnp.maximum(s[:, :HEAD], s[:, HEAD:]))
 
+    peak[mine_rows, :] = jnp.maximum(
+        peak[mine_rows, :], jnp.broadcast_to(jnp.max(new, axis=1, keepdims=True), (QUERIES, HEAD))
+    )
+
     for r in range(ROWS):
         at = pl.ds(r * QUERIES, QUERIES)
         top = jnp.max(peak[at, :], axis=1, keepdims=True)
         peak[at, :] = jnp.broadcast_to(top, (QUERIES, HEAD))
 
-    p = jnp.exp2(new - peak[mine_rows, :][:, :QUERIES])
-    acc[mine_rows, :] = jnp.dot(
-        p.astype(jnp.bfloat16), sv_ref[...], preferred_element_type=jnp.float32
-    )
-    first = lax.broadcasted_iota(jnp.int32, (QUERIES, HEAD), 1) == 0
-    total[mine_rows, :] = jnp.where(first, jnp.sum(p, axis=1, keepdims=True), 0.0)
-
     for b in range(LOCAL_BLOCKS):
-        if b % (LOCAL_BLOCKS // PARTS) == 0:
-            v_parts[b // (LOCAL_BLOCKS // PARTS)].wait()
+        if b == 0:
+            fetched.wait()
         rows, _ = rows_of(b)
         top = peak[rows, :]
         s = scores[b]
@@ -163,6 +150,13 @@
         acc[rows, :] += jnp.dot(
             p, v_ref[pl.ds(b * BLOCK, BLOCK), :], preferred_element_type=jnp.float32
         )
+
+    p = jnp.exp2(new - peak[mine_rows, :][:, :QUERIES])
+    acc[mine_rows, :] += jnp.dot(
+        p.astype(jnp.bfloat16), sv_ref[...], preferred_element_type=jnp.float32
+    )
+    first = lax.broadcasted_iota(jnp.int32, (QUERIES, HEAD), 1) == 0
+    total[mine_rows, :] += jnp.where(first, jnp.sum(p, axis=1, keepdims=True), 0.0)
 
     place = lax.broadcasted_iota(jnp.int32, (QUERIES, HEAD), 1)
     for r in range(ROWS):
@@ -175,20 +169,42 @@
                 jnp.where(place == 0, peak[at, :], one),
                 jnp.where(place == 2, peak[after, :], two),
             )
-    for at, chunk, inside in pieces(found):
-        out_ref[chunk, pl.ds(inside, 4), :] = acc[pl.ds(at, 4), :]
-        if inside < 8:
-            out_ref[chunk, pl.ds(16 + inside, 4), :] = total[pl.ds(at, 4), :]
+    for core, refs in enumerate(((keep_ref, send_ref), (send_ref, keep_ref))):
+
+        @pl.when(me % 2 == core)
+        def _():
+            for at, chunk, inside in pieces(found):
+                side = refs[at // 4 % 2]
+                side[chunk >> 1, pl.ds(inside, 4), :] = acc[pl.ds(at, 4), :]
+                if inside < 8:
+                    side[chunk >> 1, pl.ds(16 + inside, 4), :] = total[pl.ds(at, 4), :]
+
+
+def pair(one_ref, two_ref, out_ref):
+    lane = lax.broadcasted_iota(jnp.int32, (8, HEAD), 1)
+    for j in range(CHIPS):
+        one, two = one_ref[j, pl.ds(16, 8), :], two_ref[j, pl.ds(16, 8), :]
+        side = jnp.zeros((8, HEAD), jnp.float32)
+        for half in range(2):
+            at = 2 * half
+            top = jnp.maximum(one[:, at : at + 1], two[:, at : at + 1])
+            w_one = jnp.exp2(one[:, at : at + 1] - top)
+            w_two = jnp.exp2(two[:, at : at + 1] - top)
+            amount = w_one * one[:, at + 1 : at + 2] + w_two * two[:, at + 1 : at + 2]
+            rows = pl.ds(8 * half, 8)
+            out_ref[j, rows, :] = w_one * one_ref[j, rows, :] + w_two * two_ref[j, rows, :]
+            side = jnp.where(lane == at, top, jnp.where(lane == at + 1, amount, side))
+        out_ref[j, pl.ds(16, 8), :] = side
 
 
 def combine(in_ref, out_ref):
     for half in range(2):
-        sides = [in_ref[j, pl.ds(16, 8), :] for j in range(SHARDS)]
+        sides = [in_ref[j, pl.ds(16, 8), :] for j in range(CHIPS)]
         maxima = [side[:, 2 * half : 2 * half + 1] for side in sides]
         top = functools.reduce(jnp.maximum, maxima)
         numer = jnp.zeros((8, HEAD), jnp.float32)
         denom = jnp.zeros((8, 1), jnp.float32)
-        for j in range(SHARDS):
+        for j in range(CHIPS):
             w = jnp.exp2(maxima[j] - top)
             numer += w * in_ref[j, pl.ds(8 * half, 8), :]
             denom += w * sides[j][:, 2 * half + 1 : 2 * half + 2]
@@ -228,11 +244,12 @@
     q = lax.all_to_all(
         jnp.broadcast_to(q[None], (SHARDS, 16, HEAD)), "kv", split_axis=0, concat_axis=0, tiled=True
     )
-    partial = pl.pallas_call(
+    half = jax.ShapeDtypeStruct((CHIPS, CHUNK, HEAD), jnp.float32)
+    keep, send = pl.pallas_call(
         attend,
-        out_shape=jax.ShapeDtypeStruct((SHARDS, CHUNK, HEAD), jnp.float32),
+        out_shape=(half, half),
         in_specs=[vmem, vmem, vmem, vmem, hbm, hbm, vmem, vmem],
-        out_specs=vmem,
+        out_specs=(vmem, vmem),
         scratch_shapes=[
             pltpu.SMEM((2, LOCAL_BLOCKS), jnp.int32),
             pltpu.SMEM((ROWS,), jnp.int32),
@@ -246,12 +263,28 @@
             pltpu.VMEM((ROWS * QUERIES, HEAD), jnp.float32),
             pltpu.SemaphoreType.DMA((2,)),
             pltpu.SemaphoreType.DMA,
-            pltpu.SemaphoreType.DMA((PARTS,)),
+            pltpu.SemaphoreType.DMA,
         ],
         compiler_params=pltpu.CompilerParams(vmem_limit_bytes=GRANT),
         name="attend",
     )(table, limits, q, early, all_keys, all_values, new_keys, new_values)
-    moved = lax.all_to_all(partial, "kv", split_axis=0, concat_axis=0, tiled=True)
+    got = lax.ppermute(send, "kv", [(k, k ^ 1) for k in range(SHARDS)])
+    partial = pl.pallas_call(
+        pair,
+        out_shape=half,
+        in_specs=[vmem, vmem],
+        out_specs=vmem,
+        compiler_params=pltpu.CompilerParams(vmem_limit_bytes=8 * 1024 * 1024),
+        name="pair",
+    )(keep, got)
+    moved = lax.all_to_all(
+        partial,
+        "kv",
+        split_axis=0,
+        concat_axis=0,
+        tiled=True,
+        axis_index_groups=[[2 * g + core for g in range(CHIPS)] for core in range(2)],
+    )
     mine = pl.pallas_call(
         combine,
         out_shape=jax.ShapeDtypeStruct((4, 4, HEAD), jnp.float32),

time: 50.1 us -> 49.4 us (0.986)
  blocking collectives: 27 us -> 24.8 us
  waiting for transfers between devices: 14.6 us -> 15.8 us
    all_to_all x1, blocking collectives: 13.8 us -> 11.5 us  [on_device(): lax.all_to_all(partial, 'kv', split_axis=0, concat_axis=0, tiled=True, ax...]
    ppermute x0 -> x1, waiting for transfers between devices: none -> 1.33 us  [on_device(): got = lax.ppermute(send, 'kv', [(k, k ^ 1) for k in range(SHARDS)])]
    pallas_call x1 -> x2, Pallas kernels: 3.57 us -> 3.71 us  [the longest x1 2.92 us: on_device(): pl.pallas_call(attend, out_shape=(half, half), in_specs=[vmem, vmem, vmem...]
  transfers between devices with their start and end apart: 2 -> 3, of which waited for: 2 -> 3; matrix products, arithmetic and copies ran while one was open for 0% -> 0% of each run, Pallas kernels for 3% -> 4%
where the time goes in v3:
time: 49.4 us; the launch traced here: 49.2 us
  blocking collectives  24.8 us (50%)
  waiting for transfers between devices  15.8 us (32%)
  Pallas kernels  5.72 us (12%)
  starting transfers between devices  2.3 us (5%)
  local copies, waits for them, and re-layouts  0.62 us (1%)
    all_to_all x1, blocking collectives, on_device(): lax.all_to_all(jnp.broadcast_to(q[None], (SHARDS, 16, HEAD)), 'kv', split...  13.2 us
    all_to_all x1, blocking collectives, on_device(): lax.all_to_all(partial, 'kv', split_axis=0, concat_axis=0, tiled=True, ax...  11.5 us
    ppermute x1, waiting for transfers between devices, on_device(): return lax.ppermute(mine, axes, [(t, s) for s, t in gather])  9.07 us
    ppermute x1, waiting for transfers between devices, on_device(): q = lax.ppermute(queries.reshape(16, HEAD), axes, gather)  5.39 us
    pallas_call x1, Pallas kernels, on_device(): pl.pallas_call(attend, out_shape=(half, half), in_specs=[vmem, vmem, vmem...  2.92 us
    ppermute x1, starting transfers between devices, on_device(): q = lax.ppermute(queries.reshape(16, HEAD), axes, gather)  2.03 us
    pallas_call x1, Pallas kernels, on_device(): pl.pallas_call(fetch, out_shape=tuple((jax.ShapeDtypeStruct((EARLY * BLOC...  1.83 us
    ppermute x1, waiting for transfers between devices, on_device(): got = lax.ppermute(send, 'kv', [(k, k ^ 1) for k in range(SHARDS)])  1.33 us
  transfers between devices with their start and end apart: 3, of which 3 were waited for; matrix products, arithmetic and copies ran while one was open for 0% of the time, Pallas kernels for 4%

profile of v3, /device:TPU:224, one launch (start us, length us, event | category | flops | bytes accessed | tf_op | source)
XLA Modules:
  0.0 49.2 jit_solution(18367199949435720633)
XLA Ops:
  0.0 2.0 %collective-permute-start = (bf16[16,128]{1,0:T(8,128)(2,1)}, bf16[16,128]{1,0:T(8,128)(2,1)S(1)}, u32[]{:S(2)}, u32[]{:S(2)}) collective-permute-start(bf16[16,128]{1,0:T(8,128)(2,1)} %bitcast.10), channel_id=1, source_target_pairs={{0,176},{1,112},{2,48},{3,64},{4,0},{5,192},{6,128},{7,240},{8,184... | collective-permute-start | bytes 12296 | tf_op jit(solution)/shard_map/ppermute | solution.py:221
  2.0 1.8 %fetch.1 = (bf16[10752,128]{1,0:T(8,128)(2,1)S(1)}, bf16[32,128]{1,0:T(8,128)(2,1)S(1)}, bf16[32,128]{1,0:T(8,128)(2,1)S(1)}, s32[2,48]{1,0:T(2,128)S(1)}, s32[16]{0:T(128)S(1)}) custom-call(bf16[12288,128]{1,0:T(8,128)(2,1)} %bitcast.5, bf16[32,128]{1,0:T(8,128)(2,1)} %bitcast.8, bf16[32,128]{1,0:T(8,128)(2,1)} %bitcast.9, s32[2,48]{1,0:T(2,128)} %refs_3_.1, ...), custom_call_target="tpu_custom_call" | custom-call | tf_op jit(solution)/shard_map/fetch/pallas_call | solution.py:231
  3.9 5.4 %collective-permute-done = bf16[16,128]{1,0:T(8,128)(2,1)S(1)} collective-permute-done((bf16[16,128]{1,0:T(8,128)(2,1)}, bf16[16,128]{1,0:T(8,128)(2,1)S(1)}, u32[]{:S(2)}, u32[]{:S(2)}) %collective-permute-start) | collective-permute-done | bytes 4128 | tf_op jit(solution)/shard_map/ppermute | solution.py:221
  9.3 13.2 %all_to_all.10.q_ref = bf16[32,16,128]{2,1,0:T(8,128)(2,1)S(1)} all-to-all(bf16[32,16,128]{2,1,0:T(8,128)(2,1)S(1)} %broadcast_in_dim.2), channel_id=1, replica_groups=mesh['kv'=32,'head'=8] {'kv'}, dimensions={0} | all-to-all | bytes 262144 | tf_op jit(solution)/shard_map/all_to_all | solution.py:244
  22.5 2.9 %attend.1 = (f32[16,24,128]{2,1,0:T(8,128)S(1)}, f32[16,24,128]{2,1,0:T(8,128)S(1)}) custom-call(s32[2,48]{1,0:T(2,128)S(1)} %get-tuple-element.14.table_vmem, s32[16]{0:T(128)S(1)} %get-tuple-element.15.lengths_vmem, bf16[32,16,128]{2,1,0:T(8,128)(2,1)S(1)} %all_to_all.10.q_ref, bf16[10752,128]{1,0:T(8,128)(2,1)S(1)} %get-tuple-element.18.early_ref, ...), custom_call_target="tpu_custom_call" | custom-call | tf_op jit(solution)/shard_map/attend/pallas_call | solution.py:248
  25.4 0.2 collective-permute-start.1
  25.6 1.3 %collective-permute-done.1.two_ref = f32[16,24,128]{2,1,0:T(8,128)S(1)} collective-permute-done((f32[16,24,128]{2,1,0:T(8,128)S(1)}, f32[16,24,128]{2,1,0:T(8,128)S(1)}, u32[]{:S(2)}, u32[]{:S(2)}) %collective-permute-start.1) | collective-permute-done | bytes 196640 | tf_op jit(solution)/shard_map/ppermute | solution.py:271
  26.9 0.8 %pair.1 = f32[16,24,128]{2,1,0:T(8,128)S(1)} custom-call(f32[16,24,128]{2,1,0:T(8,128)S(1)} %get-tuple-element.21.one_ref, f32[16,24,128]{2,1,0:T(8,128)S(1)} %collective-permute-done.1.two_ref), custom_call_target="tpu_custom_call" | custom-call | tf_op jit(solution)/shard_map/pair/pallas_call | solution.py:272
  27.7 11.5 %all_to_all.11.in_ref = f32[16,24,128]{2,1,0:T(8,128)S(1)} all-to-all(f32[16,24,128]{2,1,0:T(8,128)S(1)} %pair.1), channel_id=1, replica_groups={{0,16,32,48,64,80,96,112,128,144,160,176,192,208,224,240},{8,24,40,56,7..., dimensions={0} | all-to-all | bytes 393216 | tf_op jit(solution)/shard_map/all_to_all | solution.py:280
  39.3 0.2 combine.1
  39.5 0.1 collective-permute-start.2
  39.5 9.1 %collective-permute-done.2 = f32[4,4,128]{2,1,0:T(4,128)S(1)} collective-permute-done((f32[4,4,128]{2,1,0:T(4,128)S(1)}, f32[4,4,128]{2,1,0:T(4,128)S(1)}, u32[]{:S(2)}, u32[]{:S(2)}) %collective-permute-start.2) | collective-permute-done | bytes 8224 | tf_op jit(solution)/shard_map/ppermute | solution.py:296
  48.6 0.6 %copy.9 = f32[4,4,128]{2,1,0:T(4,128)} copy(f32[4,4,128]{2,1,0:T(4,128)S(1)} %collective-permute-done.2) | data formatting | bytes 16384
  (1 shorter events, 0.0 us)
Async XLA Ops:
  0.0 9.2 %collective-permute-start = (bf16[16,128]{1,0:T(8,128)(2,1)}, bf16[16,128]{1,0:T(8,128)(2,1)S(1)}, u32[]{:S(2)}, u32[]{:S(2)}) collective-permute-start(bf16[16,128]{1,0:T(8,128)(2,1)} %bitcast.10), channel_id=1, source_target_pairs={{0,176},{1,112},{2,48},{3,64},{4,0},{5,192},{6,128},{7,240},{8,184... | collective-permute-start | bytes 12296 | tf_op jit(solution)/shard_map/ppermute | solution.py:221
  25.4 1.5 %collective-permute-start.1 = (f32[16,24,128]{2,1,0:T(8,128)S(1)}, f32[16,24,128]{2,1,0:T(8,128)S(1)}, u32[]{:S(2)}, u32[]{:S(2)}) collective-permute-start(f32[16,24,128]{2,1,0:T(8,128)S(1)} %get-tuple-element.22), channel_id=1, source_target_pairs={{0,8},{8,0},{16,24},{24,16},{32,40},{40,32},{48,56},{56,48},{64,72... | collective-permute-start | bytes 589832 | tf_op jit(solution)/shard_map/ppermute | solution.py:271
  39.5 9.2 %collective-permute-start.2 = (f32[4,4,128]{2,1,0:T(4,128)S(1)}, f32[4,4,128]{2,1,0:T(4,128)S(1)}, u32[]{:S(2)}, u32[]{:S(2)}) collective-permute-start(f32[4,4,128]{2,1,0:T(4,128)S(1)} %combine.1), channel_id=1, source_target_pairs={{176,0},{112,1},{48,2},{64,3},{0,4},{192,5},{128,6},{240,7},{184,8... | collective-permute-start | bytes 24584 | tf_op jit(solution)/shard_map/ppermute | solution.py:296

commit v4 on v3

--- a/solution.py
+++ b/solution.py
@@ -181,20 +181,18 @@
 
 
 def pair(one_ref, two_ref, out_ref):
-    lane = lax.broadcasted_iota(jnp.int32, (8, HEAD), 1)
+    odd = lax.broadcasted_iota(jnp.int32, (8, HEAD), 1) % 2 == 1
     for j in range(CHIPS):
         one, two = one_ref[j, pl.ds(16, 8), :], two_ref[j, pl.ds(16, 8), :]
-        side = jnp.zeros((8, HEAD), jnp.float32)
+        top = jnp.maximum(one, two)
+        w_one, w_two = jnp.exp2(one - top), jnp.exp2(two - top)
+        amount = pltpu.roll(w_one, 1, 1) * one + pltpu.roll(w_two, 1, 1) * two
+        out_ref[j, pl.ds(16, 8), :] = jnp.where(odd, amount, top)
         for half in range(2):
-            at = 2 * half
-            top = jnp.maximum(one[:, at : at + 1], two[:, at : at + 1])
-            w_one = jnp.exp2(one[:, at : at + 1] - top)
-            w_two = jnp.exp2(two[:, at : at + 1] - top)
-            amount = w_one * one[:, at + 1 : at + 2] + w_two * two[:, at + 1 : at + 2]
-            rows = pl.ds(8 * half, 8)
-            out_ref[j, rows, :] = w_one * one_ref[j, rows, :] + w_two * two_ref[j, rows, :]
-            side = jnp.where(lane == at, top, jnp.where(lane == at + 1, amount, side))
-        out_ref[j, pl.ds(16, 8), :] = side
+            rows, at = pl.ds(8 * half, 8), 2 * half
+            out_ref[j, rows, :] = (
+                w_one[:, at : at + 1] * one_ref[j, rows, :] + w_two[:, at : at + 1] * two_ref[j, rows, :]
+            )
 
 
 def combine(in_ref, out_ref):

time: 49.4 us -> 48.8 us (0.988)
  Pallas kernels: 5.72 us -> 5.15 us
    pallas_call x1, Pallas kernels: 0.79 us -> 0.22 us  [on_device(): pl.pallas_call(pair, out_shape=half, in_specs=[vmem, vmem], out_specs=vme...]
where the time goes in v4:
time: 48.8 us; the launch traced here: 48.6 us
  blocking collectives  24.8 us (51%)
  waiting for transfers between devices  15.8 us (32%)
  Pallas kernels  5.15 us (11%)
  starting transfers between devices  2.3 us (5%)
  local copies, waits for them, and re-layouts  0.62 us (1%)
    all_to_all x1, blocking collectives, on_device(): lax.all_to_all(jnp.broadcast_to(q[None], (SHARDS, 16, HEAD)), 'kv', split...  13.2 us
    all_to_all x1, blocking collectives, on_device(): lax.all_to_all(partial, 'kv', split_axis=0, concat_axis=0, tiled=True, ax...  11.5 us
    ppermute x1, waiting for transfers between devices, on_device(): return lax.ppermute(mine, axes, [(t, s) for s, t in gather])  9.07 us
    ppermute x1, waiting for transfers between devices, on_device(): q = lax.ppermute(queries.reshape(16, HEAD), axes, gather)  5.39 us
    pallas_call x1, Pallas kernels, on_device(): pl.pallas_call(attend, out_shape=(half, half), in_specs=[vmem, vmem, vmem...  2.92 us
    ppermute x1, starting transfers between devices, on_device(): q = lax.ppermute(queries.reshape(16, HEAD), axes, gather)  2.03 us
    pallas_call x1, Pallas kernels, on_device(): pl.pallas_call(fetch, out_shape=tuple((jax.ShapeDtypeStruct((EARLY * BLOC...  1.83 us
    ppermute x1, waiting for transfers between devices, on_device(): got = lax.ppermute(send, 'kv', [(k, k ^ 1) for k in range(SHARDS)])  1.33 us
  transfers between devices with their start and end apart: 3, of which 3 were waited for; matrix products, arithmetic and copies ran while one was open for 0% of the time, Pallas kernels for 4%

profile of v4, /device:TPU:224, one launch (start us, length us, event | category | flops | bytes accessed | tf_op | source)
XLA Modules:
  0.0 48.6 jit_solution(13242066836710691186)
XLA Ops:
  0.0 2.0 %collective-permute-start = (bf16[16,128]{1,0:T(8,128)(2,1)}, bf16[16,128]{1,0:T(8,128)(2,1)S(1)}, u32[]{:S(2)}, u32[]{:S(2)}) collective-permute-start(bf16[16,128]{1,0:T(8,128)(2,1)} %bitcast.10), channel_id=1, source_target_pairs={{0,176},{1,112},{2,48},{3,64},{4,0},{5,192},{6,128},{7,240},{8,184... | collective-permute-start | bytes 12296 | tf_op jit(solution)/shard_map/ppermute | solution.py:219
  2.0 1.8 %fetch.1 = (bf16[10752,128]{1,0:T(8,128)(2,1)S(1)}, bf16[32,128]{1,0:T(8,128)(2,1)S(1)}, bf16[32,128]{1,0:T(8,128)(2,1)S(1)}, s32[2,48]{1,0:T(2,128)S(1)}, s32[16]{0:T(128)S(1)}) custom-call(bf16[12288,128]{1,0:T(8,128)(2,1)} %bitcast.5, bf16[32,128]{1,0:T(8,128)(2,1)} %bitcast.8, bf16[32,128]{1,0:T(8,128)(2,1)} %bitcast.9, s32[2,48]{1,0:T(2,128)} %refs_3_.1, ...), custom_call_target="tpu_custom_call" | custom-call | tf_op jit(solution)/shard_map/fetch/pallas_call | solution.py:229
  3.9 5.4 %collective-permute-done = bf16[16,128]{1,0:T(8,128)(2,1)S(1)} collective-permute-done((bf16[16,128]{1,0:T(8,128)(2,1)}, bf16[16,128]{1,0:T(8,128)(2,1)S(1)}, u32[]{:S(2)}, u32[]{:S(2)}) %collective-permute-start) | collective-permute-done | bytes 4128 | tf_op jit(solution)/shard_map/ppermute | solution.py:219
  9.3 13.2 %all_to_all.10.q_ref = bf16[32,16,128]{2,1,0:T(8,128)(2,1)S(1)} all-to-all(bf16[32,16,128]{2,1,0:T(8,128)(2,1)S(1)} %broadcast_in_dim.2), channel_id=1, replica_groups=mesh['kv'=32,'head'=8] {'kv'}, dimensions={0} | all-to-all | bytes 262144 | tf_op jit(solution)/shard_map/all_to_all | solution.py:242
  22.5 2.9 %attend.1 = (f32[16,24,128]{2,1,0:T(8,128)S(1)}, f32[16,24,128]{2,1,0:T(8,128)S(1)}) custom-call(s32[2,48]{1,0:T(2,128)S(1)} %get-tuple-element.14.table_vmem, s32[16]{0:T(128)S(1)} %get-tuple-element.15.lengths_vmem, bf16[32,16,128]{2,1,0:T(8,128)(2,1)S(1)} %all_to_all.10.q_ref, bf16[10752,128]{1,0:T(8,128)(2,1)S(1)} %get-tuple-element.18.early_ref, ...), custom_call_target="tpu_custom_call" | custom-call | tf_op jit(solution)/shard_map/attend/pallas_call | solution.py:246
  25.4 0.2 collective-permute-start.1
  25.6 1.3 %collective-permute-done.1.two_ref = f32[16,24,128]{2,1,0:T(8,128)S(1)} collective-permute-done((f32[16,24,128]{2,1,0:T(8,128)S(1)}, f32[16,24,128]{2,1,0:T(8,128)S(1)}, u32[]{:S(2)}, u32[]{:S(2)}) %collective-permute-start.1) | collective-permute-done | bytes 196640 | tf_op jit(solution)/shard_map/ppermute | solution.py:269
  26.9 0.2 pair.1
  27.2 11.5 %all_to_all.11.in_ref = f32[16,24,128]{2,1,0:T(8,128)S(1)} all-to-all(f32[16,24,128]{2,1,0:T(8,128)S(1)} %pair.1), channel_id=1, replica_groups={{0,16,32,48,64,80,96,112,128,144,160,176,192,208,224,240},{8,24,40,56,7..., dimensions={0} | all-to-all | bytes 393216 | tf_op jit(solution)/shard_map/all_to_all | solution.py:278
  38.7 0.2 combine.1
  38.9 0.1 collective-permute-start.2
  39.0 9.1 %collective-permute-done.2 = f32[4,4,128]{2,1,0:T(4,128)S(1)} collective-permute-done((f32[4,4,128]{2,1,0:T(4,128)S(1)}, f32[4,4,128]{2,1,0:T(4,128)S(1)}, u32[]{:S(2)}, u32[]{:S(2)}) %collective-permute-start.2) | collective-permute-done | bytes 8224 | tf_op jit(solution)/shard_map/ppermute | solution.py:294
  48.0 0.6 %copy.9 = f32[4,4,128]{2,1,0:T(4,128)} copy(f32[4,4,128]{2,1,0:T(4,128)S(1)} %collective-permute-done.2) | data formatting | bytes 16384
  (1 shorter events, 0.0 us)
Async XLA Ops:
  0.0 9.2 %collective-permute-start = (bf16[16,128]{1,0:T(8,128)(2,1)}, bf16[16,128]{1,0:T(8,128)(2,1)S(1)}, u32[]{:S(2)}, u32[]{:S(2)}) collective-permute-start(bf16[16,128]{1,0:T(8,128)(2,1)} %bitcast.10), channel_id=1, source_target_pairs={{0,176},{1,112},{2,48},{3,64},{4,0},{5,192},{6,128},{7,240},{8,184... | collective-permute-start | bytes 12296 | tf_op jit(solution)/shard_map/ppermute | solution.py:219
  25.4 1.5 %collective-permute-start.1 = (f32[16,24,128]{2,1,0:T(8,128)S(1)}, f32[16,24,128]{2,1,0:T(8,128)S(1)}, u32[]{:S(2)}, u32[]{:S(2)}) collective-permute-start(f32[16,24,128]{2,1,0:T(8,128)S(1)} %get-tuple-element.22), channel_id=1, source_target_pairs={{0,8},{8,0},{16,24},{24,16},{32,40},{40,32},{48,56},{56,48},{64,72... | collective-permute-start | bytes 589832 | tf_op jit(solution)/shard_map/ppermute | solution.py:269
  38.9 9.2 %collective-permute-start.2 = (f32[4,4,128]{2,1,0:T(4,128)S(1)}, f32[4,4,128]{2,1,0:T(4,128)S(1)}, u32[]{:S(2)}, u32[]{:S(2)}) collective-permute-start(f32[4,4,128]{2,1,0:T(4,128)S(1)} %combine.1), channel_id=1, source_target_pairs={{176,0},{112,1},{48,2},{64,3},{0,4},{192,5},{128,6},{240,7},{184,8... | collective-permute-start | bytes 24584 | tf_op jit(solution)/shard_map/ppermute | solution.py:294

commit v5 on v4

--- a/solution.py
+++ b/solution.py
@@ -34,7 +34,7 @@
     right = b >> 1
     x = (2 * (c & 1) + right + (2 * right - 1) * SIDEWAYS[step]) % 4
     y = ((c >> 1) + UPWARDS[step]) % 4
-    return y * 8 + x * 2 + (b & 1)
+    return y * 8 + x * 2 + 1 - (b & 1)
 
 
 def stations():
@@ -48,7 +48,7 @@
         for right in range(2):
             x = (2 * (c & 1) + right + (2 * right - 1) * ((sideways >> step) & 1)) & 3
             for core in range(2):
-                found[h, 2 * right + core] = y * 8 + x * 2 + core
+                found[h, 2 * right + core] = y * 8 + x * 2 + 1 - core
     return found
 
 
@@ -169,7 +169,7 @@
                 jnp.where(place == 0, peak[at, :], one),
                 jnp.where(place == 2, peak[after, :], two),
             )
-    for core, refs in enumerate(((keep_ref, send_ref), (send_ref, keep_ref))):
+    for core, refs in enumerate(((send_ref, keep_ref), (keep_ref, send_ref))):
 
         @pl.when(me % 2 == core)
         def _():

time: 48.8 us -> 47.7 us (0.977)
  waiting for transfers between devices: 15.8 us -> 15.2 us
  starting transfers between devices: 2.3 us -> 1.73 us
    ppermute x1, waiting for transfers between devices: 9.07 us -> 8.49 us  [on_device(): return lax.ppermute(mine, axes, [(t, s) for s, t in gather])]
    ppermute x1, starting transfers between devices: 2.03 us -> 1.46 us  [on_device(): q = lax.ppermute(queries.reshape(16, HEAD), axes, gather)]
where the time goes in v5:
time: 47.7 us; the launch traced here: 47.5 us
  blocking collectives  24.7 us (52%)
  waiting for transfers between devices  15.2 us (32%)
  Pallas kernels  5.16 us (11%)
  starting transfers between devices  1.73 us (4%)
  local copies, waits for them, and re-layouts  0.62 us (1%)
    all_to_all x1, blocking collectives, on_device(): lax.all_to_all(jnp.broadcast_to(q[None], (SHARDS, 16, HEAD)), 'kv', split...  13.2 us
    all_to_all x1, blocking collectives, on_device(): lax.all_to_all(partial, 'kv', split_axis=0, concat_axis=0, tiled=True, ax...  11.5 us
    ppermute x1, waiting for transfers between devices, on_device(): return lax.ppermute(mine, axes, [(t, s) for s, t in gather])  8.49 us
    ppermute x1, waiting for transfers between devices, on_device(): q = lax.ppermute(queries.reshape(16, HEAD), axes, gather)  5.4 us
    pallas_call x1, Pallas kernels, on_device(): pl.pallas_call(attend, out_shape=(half, half), in_specs=[vmem, vmem, vmem...  2.93 us
    pallas_call x1, Pallas kernels, on_device(): pl.pallas_call(fetch, out_shape=tuple((jax.ShapeDtypeStruct((EARLY * BLOC...  1.83 us
    ppermute x1, starting transfers between devices, on_device(): q = lax.ppermute(queries.reshape(16, HEAD), axes, gather)  1.46 us
    ppermute x1, waiting for transfers between devices, on_device(): got = lax.ppermute(send, 'kv', [(k, k ^ 1) for k in range(SHARDS)])  1.34 us
  transfers between devices with their start and end apart: 3, of which 3 were waited for; matrix products, arithmetic and copies ran while one was open for 0% of the time, Pallas kernels for 4%

profile of v5, /device:TPU:224, one launch (start us, length us, event | category | flops | bytes accessed | tf_op | source)
XLA Modules:
  0.0 47.5 jit_solution(3430643629809856960)
XLA Ops:
  0.0 1.5 %collective-permute-start = (bf16[16,128]{1,0:T(8,128)(2,1)}, bf16[16,128]{1,0:T(8,128)(2,1)S(1)}, u32[]{:S(2)}, u32[]{:S(2)}) collective-permute-start(bf16[16,128]{1,0:T(8,128)(2,1)} %bitcast.10), channel_id=1, source_target_pairs={{0,184},{1,120},{2,56},{3,72},{4,8},{5,200},{6,136},{7,248},{8,176... | collective-permute-start | bytes 12296 | tf_op jit(solution)/shard_map/ppermute | solution.py:219
  1.5 1.8 %fetch.1 = (bf16[10752,128]{1,0:T(8,128)(2,1)S(1)}, bf16[32,128]{1,0:T(8,128)(2,1)S(1)}, bf16[32,128]{1,0:T(8,128)(2,1)S(1)}, s32[2,48]{1,0:T(2,128)S(1)}, s32[16]{0:T(128)S(1)}) custom-call(bf16[12288,128]{1,0:T(8,128)(2,1)} %bitcast.5, bf16[32,128]{1,0:T(8,128)(2,1)} %bitcast.8, bf16[32,128]{1,0:T(8,128)(2,1)} %bitcast.9, s32[2,48]{1,0:T(2,128)} %refs_3_.1, ...), custom_call_target="tpu_custom_call" | custom-call | tf_op jit(solution)/shard_map/fetch/pallas_call | solution.py:229
  3.3 5.4 %collective-permute-done = bf16[16,128]{1,0:T(8,128)(2,1)S(1)} collective-permute-done((bf16[16,128]{1,0:T(8,128)(2,1)}, bf16[16,128]{1,0:T(8,128)(2,1)S(1)}, u32[]{:S(2)}, u32[]{:S(2)}) %collective-permute-start) | collective-permute-done | bytes 4128 | tf_op jit(solution)/shard_map/ppermute | solution.py:219
  8.7 13.2 %all_to_all.10.q_ref = bf16[32,16,128]{2,1,0:T(8,128)(2,1)S(1)} all-to-all(bf16[32,16,128]{2,1,0:T(8,128)(2,1)S(1)} %broadcast_in_dim.2), channel_id=1, replica_groups=mesh['kv'=32,'head'=8] {'kv'}, dimensions={0} | all-to-all | bytes 262144 | tf_op jit(solution)/shard_map/all_to_all | solution.py:242
  21.9 2.9 %attend.1 = (f32[16,24,128]{2,1,0:T(8,128)S(1)}, f32[16,24,128]{2,1,0:T(8,128)S(1)}) custom-call(s32[2,48]{1,0:T(2,128)S(1)} %get-tuple-element.14.table_vmem, s32[16]{0:T(128)S(1)} %get-tuple-element.15.lengths_vmem, bf16[32,16,128]{2,1,0:T(8,128)(2,1)S(1)} %all_to_all.10.q_ref, bf16[10752,128]{1,0:T(8,128)(2,1)S(1)} %get-tuple-element.18.early_ref, ...), custom_call_target="tpu_custom_call" | custom-call | tf_op jit(solution)/shard_map/attend/pallas_call | solution.py:246
  24.9 0.2 collective-permute-start.1
  25.1 1.3 %collective-permute-done.1.two_ref = f32[16,24,128]{2,1,0:T(8,128)S(1)} collective-permute-done((f32[16,24,128]{2,1,0:T(8,128)S(1)}, f32[16,24,128]{2,1,0:T(8,128)S(1)}, u32[]{:S(2)}, u32[]{:S(2)}) %collective-permute-start.1) | collective-permute-done | bytes 196640 | tf_op jit(solution)/shard_map/ppermute | solution.py:269
  26.4 0.2 pair.1
  26.6 11.5 %all_to_all.11.in_ref = f32[16,24,128]{2,1,0:T(8,128)S(1)} all-to-all(f32[16,24,128]{2,1,0:T(8,128)S(1)} %pair.1), channel_id=1, replica_groups={{0,16,32,48,64,80,96,112,128,144,160,176,192,208,224,240},{8,24,40,56,7..., dimensions={0} | all-to-all | bytes 393216 | tf_op jit(solution)/shard_map/all_to_all | solution.py:278
  38.1 0.2 combine.1
  38.3 0.1 collective-permute-start.2
  38.4 8.5 %collective-permute-done.2 = f32[4,4,128]{2,1,0:T(4,128)S(1)} collective-permute-done((f32[4,4,128]{2,1,0:T(4,128)S(1)}, f32[4,4,128]{2,1,0:T(4,128)S(1)}, u32[]{:S(2)}, u32[]{:S(2)}) %collective-permute-start.2) | collective-permute-done | bytes 8224 | tf_op jit(solution)/shard_map/ppermute | solution.py:294
  46.9 0.6 %copy.9 = f32[4,4,128]{2,1,0:T(4,128)} copy(f32[4,4,128]{2,1,0:T(4,128)S(1)} %collective-permute-done.2) | data formatting | bytes 16384
  (1 shorter events, 0.0 us)
Async XLA Ops:
  0.0 8.7 %collective-permute-start = (bf16[16,128]{1,0:T(8,128)(2,1)}, bf16[16,128]{1,0:T(8,128)(2,1)S(1)}, u32[]{:S(2)}, u32[]{:S(2)}) collective-permute-start(bf16[16,128]{1,0:T(8,128)(2,1)} %bitcast.10), channel_id=1, source_target_pairs={{0,184},{1,120},{2,56},{3,72},{4,8},{5,200},{6,136},{7,248},{8,176... | collective-permute-start | bytes 12296 | tf_op jit(solution)/shard_map/ppermute | solution.py:219
  24.9 1.5 %collective-permute-start.1 = (f32[16,24,128]{2,1,0:T(8,128)S(1)}, f32[16,24,128]{2,1,0:T(8,128)S(1)}, u32[]{:S(2)}, u32[]{:S(2)}) collective-permute-start(f32[16,24,128]{2,1,0:T(8,128)S(1)} %get-tuple-element.22), channel_id=1, source_target_pairs={{0,8},{8,0},{16,24},{24,16},{32,40},{40,32},{48,56},{56,48},{64,72... | collective-permute-start | bytes 589832 | tf_op jit(solution)/shard_map/ppermute | solution.py:269
  38.3 8.6 %collective-permute-start.2 = (f32[4,4,128]{2,1,0:T(4,128)S(1)}, f32[4,4,128]{2,1,0:T(4,128)S(1)}, u32[]{:S(2)}, u32[]{:S(2)}) collective-permute-start(f32[4,4,128]{2,1,0:T(4,128)S(1)} %combine.1), channel_id=1, source_target_pairs={{184,0},{120,1},{56,2},{72,3},{8,4},{200,5},{136,6},{248,7},{176,8... | collective-permute-start | bytes 24584 | tf_op jit(solution)/shard_map/ppermute | solution.py:294

commit v6 on v5

--- a/solution.py
+++ b/solution.py
@@ -59,31 +59,43 @@
                 yield r * QUERIES + s * GROUP + b * 4, found[s * 4 + r // 4, b], (r % 4) * 4
 
 
-def fetch(*refs):
-    count = len(refs) // 2
+def fetch(k_hbm, sk_hbm, sv_hbm, table_hbm, lengths_hbm, early_ref, sk_ref, sv_ref, plan_ref, table, lengths, sems):
     copies = [
-        pltpu.make_async_copy(refs[i].at[pl.ds(0, refs[count + i].shape[0])], refs[count + i], refs[-1].at[i])
-        for i in range(count)
+        pltpu.make_async_copy(src, dst, sems.at[i])
+        for i, (src, dst) in enumerate(
+            [
+                (table_hbm, table),
+                (lengths_hbm, lengths),
+                (k_hbm.at[pl.ds(0, EARLY * BLOCK)], early_ref),
+                (sk_hbm, sk_ref),
+                (sv_hbm, sv_ref),
+            ]
+        )
     ]
     for copy in copies:
         copy.start()
-    for copy in copies:
+    for copy in copies[:2]:
         copy.wait()
+    row = table[pl.ds(0, 1), :]
+    limit = jnp.zeros_like(row)
+    for r in range(ROWS):
+        limit = jnp.where(row == r, lengths[r], limit)
+    plan_ref[pl.ds(0, 1), :] = jnp.maximum(row, 0) * QUERIES
+    plan_ref[pl.ds(1, 1), :] = jnp.where(row >= 0, limit - table[pl.ds(1, 1), :] * BLOCK, 0)
+    for copy in copies[2:]:
+        copy.wait()
 
 
 def attend(
-    table_vmem, lengths_vmem, q_ref, early_ref, k_hbm, v_hbm, sk_ref, sv_ref, keep_ref, send_ref,
-    table, lengths, late_ref, v_ref, wide, qs, scores, peak, total, acc, small_sems, k_sem, v_sem,
+    plan_vmem, q_ref, early_ref, k_hbm, v_hbm, sk_ref, sv_ref, keep_ref, send_ref,
+    plan, late_ref, v_ref, wide, qs, scores, peak, total, acc, plan_sem, k_sem, v_sem,
 ):
-    small = [
-        pltpu.make_async_copy(table_vmem, table, small_sems.at[0]),
-        pltpu.make_async_copy(lengths_vmem, lengths, small_sems.at[1]),
-    ]
+    planned = pltpu.make_async_copy(plan_vmem, plan, plan_sem)
     late = pltpu.make_async_copy(
         k_hbm.at[pl.ds(EARLY * BLOCK, (LOCAL_BLOCKS - EARLY) * BLOCK)], late_ref, k_sem
     )
     fetched = pltpu.make_async_copy(v_hbm, v_ref, v_sem)
-    for copy in small + [late, fetched]:
+    for copy in (planned, late, fetched):
         copy.start()
     found = stations()
     wide[...] = q_ref[...].astype(jnp.float32)
@@ -97,13 +109,10 @@
     lane = lax.broadcasted_iota(jnp.int32, (QUERIES, BLOCK), 1)
 
     def rows_of(b):
-        row = table[0, b]
-        r = jnp.maximum(row, 0)
-        live = jnp.where(row >= 0, lengths[r] - table[1, b] * BLOCK, 0)
-        return pl.ds(pl.multiple_of(r * QUERIES, QUERIES), QUERIES), live
-
-    for copy in small + [late]:
-        copy.wait()
+        return pl.ds(pl.multiple_of(plan[0, b], QUERIES), QUERIES)
+
+    planned.wait()
+
     me = lax.axis_index("kv")
     mine = jnp.minimum(me, ROWS - 1)
     mine_rows = pl.ds(pl.multiple_of(mine * QUERIES, QUERIES), QUERIES)
@@ -115,7 +124,9 @@
     )
     new = jnp.where(seen, new * SCALE, MASKED)
     for b in range(LOCAL_BLOCKS):
-        rows, live = rows_of(b)
+        if b == EARLY:
+            late.wait()
+        rows, live = rows_of(b), plan[1, b]
         s = lax.dot_general(
             qs[rows, :],
             early_ref[pl.ds(b * BLOCK, BLOCK), :]
@@ -140,7 +151,7 @@
     for b in range(LOCAL_BLOCKS):
         if b == 0:
             fetched.wait()
-        rows, _ = rows_of(b)
+        rows = rows_of(b)
         top = peak[rows, :]
         s = scores[b]
         left = jnp.exp2(s[:, :HEAD] - top)
@@ -226,15 +237,21 @@
         block_table,
         lengths,
     ]
-    early, new_keys, new_values, table, limits = pl.pallas_call(
+    early, new_keys, new_values, plan = pl.pallas_call(
         fetch,
-        out_shape=tuple(
-            jax.ShapeDtypeStruct((EARLY * BLOCK, HEAD) if i == 0 else x.shape, x.dtype)
-            for i, x in enumerate(sources)
+        out_shape=(
+            jax.ShapeDtypeStruct((EARLY * BLOCK, HEAD), jnp.bfloat16),
+            jax.ShapeDtypeStruct((STEPS * ROWS, HEAD), jnp.bfloat16),
+            jax.ShapeDtypeStruct((STEPS * ROWS, HEAD), jnp.bfloat16),
+            jax.ShapeDtypeStruct((2, LOCAL_BLOCKS), jnp.int32),
         ),
         in_specs=[hbm] * 5,
-        out_specs=(vmem,) * 5,
-        scratch_shapes=[pltpu.SemaphoreType.DMA((5,))],
+        out_specs=(vmem,) * 4,
+        scratch_shapes=[
+            pltpu.VMEM((2, LOCAL_BLOCKS), jnp.int32),
+            pltpu.SMEM((ROWS,), jnp.int32),
+            pltpu.SemaphoreType.DMA((5,)),
+        ],
         compiler_params=pltpu.CompilerParams(vmem_limit_bytes=GRANT),
         name="fetch",
     )(*[pltpu.with_memory_space_constraint(x, pltpu.HBM) for x in sources])
@@ -246,11 +263,10 @@
     keep, send = pl.pallas_call(
         attend,
         out_shape=(half, half),
-        in_specs=[vmem, vmem, vmem, vmem, hbm, hbm, vmem, vmem],
+        in_specs=[vmem, vmem, vmem, hbm, hbm, vmem, vmem],
         out_specs=(vmem, vmem),
         scratch_shapes=[
             pltpu.SMEM((2, LOCAL_BLOCKS), jnp.int32),
-            pltpu.SMEM((ROWS,), jnp.int32),
             pltpu.VMEM(((LOCAL_BLOCKS - EARLY) * BLOCK, HEAD), jnp.bfloat16),
             pltpu.VMEM((LOCAL_BLOCKS * BLOCK, HEAD), jnp.bfloat16),
             pltpu.VMEM((SHARDS, 16, HEAD), jnp.float32),
@@ -259,13 +275,13 @@
             pltpu.VMEM((ROWS * QUERIES, HEAD), jnp.float32),
             pltpu.VMEM((ROWS * QUERIES, HEAD), jnp.float32),
             pltpu.VMEM((ROWS * QUERIES, HEAD), jnp.float32),
-            pltpu.SemaphoreType.DMA((2,)),
+            pltpu.SemaphoreType.DMA,
             pltpu.SemaphoreType.DMA,
             pltpu.SemaphoreType.DMA,
         ],
         compiler_params=pltpu.CompilerParams(vmem_limit_bytes=GRANT),
         name="attend",
-    )(table, limits, q, early, all_keys, all_values, new_keys, new_values)
+    )(plan, q, early, all_keys, all_values, new_keys, new_values)
     got = lax.ppermute(send, "kv", [(k, k ^ 1) for k in range(SHARDS)])
     partial = pl.pallas_call(
         pair,

time: 47.7 us -> 47.5 us (level)
  no operation moved by 1% of the time
where the time goes in v6:
time: 47.5 us; the launch traced here: 47.3 us
  blocking collectives  24.7 us (52%)
  waiting for transfers between devices  15.2 us (32%)
  Pallas kernels  5 us (11%)
  starting transfers between devices  1.72 us (4%)
  local copies, waits for them, and re-layouts  0.62 us (1%)
    all_to_all x1, blocking collectives, on_device(): lax.all_to_all(jnp.broadcast_to(q[None], (SHARDS, 16, HEAD)), 'kv', split...  13.2 us
    all_to_all x1, blocking collectives, on_device(): lax.all_to_all(partial, 'kv', split_axis=0, concat_axis=0, tiled=True, ax...  11.5 us
    ppermute x1, waiting for transfers between devices, on_device(): return lax.ppermute(mine, axes, [(t, s) for s, t in gather])  8.49 us
    ppermute x1, waiting for transfers between devices, on_device(): q = lax.ppermute(queries.reshape(16, HEAD), axes, gather)  5.39 us
    pallas_call x1, Pallas kernels, on_device(): pl.pallas_call(attend, out_shape=(half, half), in_specs=[vmem, vmem, vmem...  2.76 us
    pallas_call x1, Pallas kernels, on_device(): pl.pallas_call(fetch, out_shape=(jax.ShapeDtypeStruct((EARLY * BLOCK, HEA...  1.84 us
    ppermute x1, starting transfers between devices, on_device(): q = lax.ppermute(queries.reshape(16, HEAD), axes, gather)  1.46 us
    ppermute x1, waiting for transfers between devices, on_device(): got = lax.ppermute(send, 'kv', [(k, k ^ 1) for k in range(SHARDS)])  1.35 us
  transfers between devices with their start and end apart: 3, of which 3 were waited for; matrix products, arithmetic and copies ran while one was open for 0% of the time, Pallas kernels for 4%

profile of v6, /device:TPU:224, one launch (start us, length us, event | category | flops | bytes accessed | tf_op | source)
XLA Modules:
  0.0 47.3 jit_solution(15289016296022052407)
XLA Ops:
  0.0 1.5 %collective-permute-start = (bf16[16,128]{1,0:T(8,128)(2,1)}, bf16[16,128]{1,0:T(8,128)(2,1)S(1)}, u32[]{:S(2)}, u32[]{:S(2)}) collective-permute-start(bf16[16,128]{1,0:T(8,128)(2,1)} %bitcast.10), channel_id=1, source_target_pairs={{0,184},{1,120},{2,56},{3,72},{4,8},{5,200},{6,136},{7,248},{8,176... | collective-permute-start | bytes 12296 | tf_op jit(solution)/shard_map/ppermute | solution.py:230
  1.5 1.8 %fetch.1 = (bf16[10752,128]{1,0:T(8,128)(2,1)S(1)}, bf16[32,128]{1,0:T(8,128)(2,1)S(1)}, bf16[32,128]{1,0:T(8,128)(2,1)S(1)}, s32[2,48]{1,0:T(2,128)S(1)}) custom-call(bf16[12288,128]{1,0:T(8,128)(2,1)} %bitcast.5, bf16[32,128]{1,0:T(8,128)(2,1)} %bitcast.8, bf16[32,128]{1,0:T(8,128)(2,1)} %bitcast.9, s32[2,48]{1,0:T(2,128)} %table_hbm.1, s32[16]{0:T(128)} %lengths_hbm.1), custom_call_target="tpu_custom_call" | custom-call | tf_op jit(solution)/shard_map/fetch/pallas_call | solution.py:240
  3.3 5.4 %collective-permute-done = bf16[16,128]{1,0:T(8,128)(2,1)S(1)} collective-permute-done((bf16[16,128]{1,0:T(8,128)(2,1)}, bf16[16,128]{1,0:T(8,128)(2,1)S(1)}, u32[]{:S(2)}, u32[]{:S(2)}) %collective-permute-start) | collective-permute-done | bytes 4128 | tf_op jit(solution)/shard_map/ppermute | solution.py:230
  8.7 13.2 %all_to_all.10.q_ref = bf16[32,16,128]{2,1,0:T(8,128)(2,1)S(1)} all-to-all(bf16[32,16,128]{2,1,0:T(8,128)(2,1)S(1)} %broadcast_in_dim.2), channel_id=1, replica_groups=mesh['kv'=32,'head'=8] {'kv'}, dimensions={0} | all-to-all | bytes 262144 | tf_op jit(solution)/shard_map/all_to_all | solution.py:259
  21.9 2.8 %attend.1 = (f32[16,24,128]{2,1,0:T(8,128)S(1)}, f32[16,24,128]{2,1,0:T(8,128)S(1)}) custom-call(s32[2,48]{1,0:T(2,128)S(1)} %get-tuple-element.13.plan_vmem, bf16[32,16,128]{2,1,0:T(8,128)(2,1)S(1)} %all_to_all.10.q_ref, bf16[10752,128]{1,0:T(8,128)(2,1)S(1)} %get-tuple-element.16.early_ref, bf16[12288,128]{1,0:T(8,128)(2,1)} %bitcast.6, ...), custom_call_target="tpu_custom_call" | custom-call | tf_op jit(solution)/shard_map/attend/pallas_call | solution.py:263
  24.7 0.2 collective-permute-start.1
  24.9 1.4 %collective-permute-done.1.two_ref = f32[16,24,128]{2,1,0:T(8,128)S(1)} collective-permute-done((f32[16,24,128]{2,1,0:T(8,128)S(1)}, f32[16,24,128]{2,1,0:T(8,128)S(1)}, u32[]{:S(2)}, u32[]{:S(2)}) %collective-permute-start.1) | collective-permute-done | bytes 196640 | tf_op jit(solution)/shard_map/ppermute | solution.py:285
  26.2 0.2 pair.1
  26.5 11.5 %all_to_all.11.in_ref = f32[16,24,128]{2,1,0:T(8,128)S(1)} all-to-all(f32[16,24,128]{2,1,0:T(8,128)S(1)} %pair.1), channel_id=1, replica_groups={{0,16,32,48,64,80,96,112,128,144,160,176,192,208,224,240},{8,24,40,56,7..., dimensions={0} | all-to-all | bytes 393216 | tf_op jit(solution)/shard_map/all_to_all | solution.py:294
  38.0 0.2 combine.1
  38.2 0.1 collective-permute-start.2
  38.2 8.5 %collective-permute-done.2 = f32[4,4,128]{2,1,0:T(4,128)S(1)} collective-permute-done((f32[4,4,128]{2,1,0:T(4,128)S(1)}, f32[4,4,128]{2,1,0:T(4,128)S(1)}, u32[]{:S(2)}, u32[]{:S(2)}) %collective-permute-start.2) | collective-permute-done | bytes 8224 | tf_op jit(solution)/shard_map/ppermute | solution.py:310
  46.7 0.6 %copy.9 = f32[4,4,128]{2,1,0:T(4,128)} copy(f32[4,4,128]{2,1,0:T(4,128)S(1)} %collective-permute-done.2) | data formatting | bytes 16384
  (1 shorter events, 0.0 us)
Async XLA Ops:
  0.0 8.7 %collective-permute-start = (bf16[16,128]{1,0:T(8,128)(2,1)}, bf16[16,128]{1,0:T(8,128)(2,1)S(1)}, u32[]{:S(2)}, u32[]{:S(2)}) collective-permute-start(bf16[16,128]{1,0:T(8,128)(2,1)} %bitcast.10), channel_id=1, source_target_pairs={{0,184},{1,120},{2,56},{3,72},{4,8},{5,200},{6,136},{7,248},{8,176... | collective-permute-start | bytes 12296 | tf_op jit(solution)/shard_map/ppermute | solution.py:230
  24.7 1.5 %collective-permute-start.1 = (f32[16,24,128]{2,1,0:T(8,128)S(1)}, f32[16,24,128]{2,1,0:T(8,128)S(1)}, u32[]{:S(2)}, u32[]{:S(2)}) collective-permute-start(f32[16,24,128]{2,1,0:T(8,128)S(1)} %get-tuple-element.20), channel_id=1, source_target_pairs={{0,8},{8,0},{16,24},{24,16},{32,40},{40,32},{48,56},{56,48},{64,72... | collective-permute-start | bytes 589832 | tf_op jit(solution)/shard_map/ppermute | solution.py:285
  38.2 8.6 %collective-permute-start.2 = (f32[4,4,128]{2,1,0:T(4,128)S(1)}, f32[4,4,128]{2,1,0:T(4,128)S(1)}, u32[]{:S(2)}, u32[]{:S(2)}) collective-permute-start(f32[4,4,128]{2,1,0:T(4,128)S(1)} %combine.1), channel_id=1, source_target_pairs={{184,0},{120,1},{56,2},{72,3},{8,4},{200,5},{136,6},{248,7},{176,8... | collective-permute-start | bytes 24584 | tf_op jit(solution)/shard_map/ppermute | solution.py:310

commit v7 on v6

--- a/solution.py
+++ b/solution.py
@@ -21,7 +21,7 @@
 MASKED = -1e30
 SCALE = math.log2(math.e) / math.sqrt(HEAD)
 CHUNK = 24
-EARLY = 42
+EARLY = 40
 GRANT = 16 * 1024 * 1024
 
 

time: 47.5 us -> 47.6 us (level)
  no operation moved by 1% of the time
where the time goes in v7:
time: 47.6 us; the launch traced here: 47.4 us
  blocking collectives  24.7 us (52%)
  waiting for transfers between devices  15.3 us (32%)
  Pallas kernels  5 us (11%)
  starting transfers between devices  1.73 us (4%)
  local copies, waits for them, and re-layouts  0.62 us (1%)
    all_to_all x1, blocking collectives, on_device(): lax.all_to_all(jnp.broadcast_to(q[None], (SHARDS, 16, HEAD)), 'kv', split...  13.2 us
    all_to_all x1, blocking collectives, on_device(): lax.all_to_all(partial, 'kv', split_axis=0, concat_axis=0, tiled=True, ax...  11.5 us
    ppermute x1, waiting for transfers between devices, on_device(): return lax.ppermute(mine, axes, [(t, s) for s, t in gather])  8.49 us
    ppermute x1, waiting for transfers between devices, on_device(): q = lax.ppermute(queries.reshape(16, HEAD), axes, gather)  5.42 us
    pallas_call x1, Pallas kernels, on_device(): pl.pallas_call(attend, out_shape=(half, half), in_specs=[vmem, vmem, vmem...  2.79 us
    pallas_call x1, Pallas kernels, on_device(): pl.pallas_call(fetch, out_shape=(jax.ShapeDtypeStruct((EARLY * BLOCK, HEA...  1.8 us
    ppermute x1, starting transfers between devices, on_device(): q = lax.ppermute(queries.reshape(16, HEAD), axes, gather)  1.46 us
    ppermute x1, waiting for transfers between devices, on_device(): got = lax.ppermute(send, 'kv', [(k, k ^ 1) for k in range(SHARDS)])  1.34 us
  transfers between devices with their start and end apart: 3, of which 3 were waited for; matrix products, arithmetic and copies ran while one was open for 0% of the time, Pallas kernels for 4%

profile of v7, /device:TPU:224, one launch (start us, length us, event | category | flops | bytes accessed | tf_op | source)
XLA Modules:
  0.0 47.4 jit_solution(11822430198465409993)
XLA Ops:
  0.0 1.5 %collective-permute-start = (bf16[16,128]{1,0:T(8,128)(2,1)}, bf16[16,128]{1,0:T(8,128)(2,1)S(1)}, u32[]{:S(2)}, u32[]{:S(2)}) collective-permute-start(bf16[16,128]{1,0:T(8,128)(2,1)} %bitcast.10), channel_id=1, source_target_pairs={{0,184},{1,120},{2,56},{3,72},{4,8},{5,200},{6,136},{7,248},{8,176... | collective-permute-start | bytes 12296 | tf_op jit(solution)/shard_map/ppermute | solution.py:230
  1.5 1.8 %fetch.1 = (bf16[10240,128]{1,0:T(8,128)(2,1)S(1)}, bf16[32,128]{1,0:T(8,128)(2,1)S(1)}, bf16[32,128]{1,0:T(8,128)(2,1)S(1)}, s32[2,48]{1,0:T(2,128)S(1)}) custom-call(bf16[12288,128]{1,0:T(8,128)(2,1)} %bitcast.5, bf16[32,128]{1,0:T(8,128)(2,1)} %bitcast.8, bf16[32,128]{1,0:T(8,128)(2,1)} %bitcast.9, s32[2,48]{1,0:T(2,128)} %table_hbm.1, s32[16]{0:T(128)} %lengths_hbm.1), custom_call_target="tpu_custom_call" | custom-call | tf_op jit(solution)/shard_map/fetch/pallas_call | solution.py:240
  3.3 5.4 %collective-permute-done = bf16[16,128]{1,0:T(8,128)(2,1)S(1)} collective-permute-done((bf16[16,128]{1,0:T(8,128)(2,1)}, bf16[16,128]{1,0:T(8,128)(2,1)S(1)}, u32[]{:S(2)}, u32[]{:S(2)}) %collective-permute-start) | collective-permute-done | bytes 4128 | tf_op jit(solution)/shard_map/ppermute | solution.py:230
  8.7 13.2 %all_to_all.10.q_ref = bf16[32,16,128]{2,1,0:T(8,128)(2,1)S(1)} all-to-all(bf16[32,16,128]{2,1,0:T(8,128)(2,1)S(1)} %broadcast_in_dim.2), channel_id=1, replica_groups=mesh['kv'=32,'head'=8] {'kv'}, dimensions={0} | all-to-all | bytes 262144 | tf_op jit(solution)/shard_map/all_to_all | solution.py:259
  21.9 2.8 %attend.1 = (f32[16,24,128]{2,1,0:T(8,128)S(1)}, f32[16,24,128]{2,1,0:T(8,128)S(1)}) custom-call(s32[2,48]{1,0:T(2,128)S(1)} %get-tuple-element.13.plan_vmem, bf16[32,16,128]{2,1,0:T(8,128)(2,1)S(1)} %all_to_all.10.q_ref, bf16[10240,128]{1,0:T(8,128)(2,1)S(1)} %get-tuple-element.16.early_ref, bf16[12288,128]{1,0:T(8,128)(2,1)} %bitcast.6, ...), custom_call_target="tpu_custom_call" | custom-call | tf_op jit(solution)/shard_map/attend/pallas_call | solution.py:263
  24.7 0.2 collective-permute-start.1
  24.9 1.3 %collective-permute-done.1.two_ref = f32[16,24,128]{2,1,0:T(8,128)S(1)} collective-permute-done((f32[16,24,128]{2,1,0:T(8,128)S(1)}, f32[16,24,128]{2,1,0:T(8,128)S(1)}, u32[]{:S(2)}, u32[]{:S(2)}) %collective-permute-start.1) | collective-permute-done | bytes 196640 | tf_op jit(solution)/shard_map/ppermute | solution.py:285
  26.3 0.2 pair.1
  26.5 11.5 %all_to_all.11.in_ref = f32[16,24,128]{2,1,0:T(8,128)S(1)} all-to-all(f32[16,24,128]{2,1,0:T(8,128)S(1)} %pair.1), channel_id=1, replica_groups={{0,16,32,48,64,80,96,112,128,144,160,176,192,208,224,240},{8,24,40,56,7..., dimensions={0} | all-to-all | bytes 393216 | tf_op jit(solution)/shard_map/all_to_all | solution.py:294
  38.0 0.2 combine.1
  38.2 0.1 collective-permute-start.2
  38.3 8.5 %collective-permute-done.2 = f32[4,4,128]{2,1,0:T(4,128)S(1)} collective-permute-done((f32[4,4,128]{2,1,0:T(4,128)S(1)}, f32[4,4,128]{2,1,0:T(4,128)S(1)}, u32[]{:S(2)}, u32[]{:S(2)}) %collective-permute-start.2) | collective-permute-done | bytes 8224 | tf_op jit(solution)/shard_map/ppermute | solution.py:310
  46.8 0.6 %copy.9 = f32[4,4,128]{2,1,0:T(4,128)} copy(f32[4,4,128]{2,1,0:T(4,128)S(1)} %collective-permute-done.2) | data formatting | bytes 16384
  (1 shorter events, 0.0 us)
Async XLA Ops:
  0.0 8.7 %collective-permute-start = (bf16[16,128]{1,0:T(8,128)(2,1)}, bf16[16,128]{1,0:T(8,128)(2,1)S(1)}, u32[]{:S(2)}, u32[]{:S(2)}) collective-permute-start(bf16[16,128]{1,0:T(8,128)(2,1)} %bitcast.10), channel_id=1, source_target_pairs={{0,184},{1,120},{2,56},{3,72},{4,8},{5,200},{6,136},{7,248},{8,176... | collective-permute-start | bytes 12296 | tf_op jit(solution)/shard_map/ppermute | solution.py:230
  24.7 1.5 %collective-permute-start.1 = (f32[16,24,128]{2,1,0:T(8,128)S(1)}, f32[16,24,128]{2,1,0:T(8,128)S(1)}, u32[]{:S(2)}, u32[]{:S(2)}) collective-permute-start(f32[16,24,128]{2,1,0:T(8,128)S(1)} %get-tuple-element.20), channel_id=1, source_target_pairs={{0,8},{8,0},{16,24},{24,16},{32,40},{40,32},{48,56},{56,48},{64,72... | collective-permute-start | bytes 589832 | tf_op jit(solution)/shard_map/ppermute | solution.py:285
  38.2 8.6 %collective-permute-start.2 = (f32[4,4,128]{2,1,0:T(4,128)S(1)}, f32[4,4,128]{2,1,0:T(4,128)S(1)}, u32[]{:S(2)}, u32[]{:S(2)}) collective-permute-start(f32[4,4,128]{2,1,0:T(4,128)S(1)} %combine.1), channel_id=1, source_target_pairs={{184,0},{120,1},{56,2},{72,3},{8,4},{200,5},{136,6},{248,7},{176,8... | collective-permute-start | bytes 24584 | tf_op jit(solution)/shard_map/ppermute | solution.py:310

commit v8 on v6

--- a/solution.py
+++ b/solution.py
@@ -207,17 +207,14 @@
 
 
 def combine(in_ref, out_ref):
+    sides = [in_ref[j, pl.ds(16, 8), :] for j in range(CHIPS)]
+    top = functools.reduce(jnp.maximum, sides)
+    weights = [jnp.exp2(side - top) for side in sides]
+    denom = sum(pltpu.roll(w, 1, 1) * side for w, side in zip(weights, sides))
     for half in range(2):
-        sides = [in_ref[j, pl.ds(16, 8), :] for j in range(CHIPS)]
-        maxima = [side[:, 2 * half : 2 * half + 1] for side in sides]
-        top = functools.reduce(jnp.maximum, maxima)
-        numer = jnp.zeros((8, HEAD), jnp.float32)
-        denom = jnp.zeros((8, 1), jnp.float32)
-        for j in range(CHIPS):
-            w = jnp.exp2(maxima[j] - top)
-            numer += w * in_ref[j, pl.ds(8 * half, 8), :]
-            denom += w * sides[j][:, 2 * half + 1 : 2 * half + 2]
-        out_ref[pl.ds(2 * half, 2)] = (numer / denom).reshape(2, 4, HEAD)
+        at = 2 * half
+        numer = sum(w[:, at : at + 1] * in_ref[j, pl.ds(8 * half, 8), :] for j, w in enumerate(weights))
+        out_ref[pl.ds(2 * half, 2)] = (numer / denom[:, at + 1 : at + 2]).reshape(2, 4, HEAD)
 
 
 def on_device(queries, keys, values, step_keys, step_values, lengths, block_table):

time: 47.5 us -> 47.5 us (level)
  no operation moved by 1% of the time
where the time goes in v8:
time: 47.5 us; the launch traced here: 47.3 us
  blocking collectives  24.7 us (52%)
  waiting for transfers between devices  15.2 us (32%)
  Pallas kernels  5 us (11%)
  starting transfers between devices  1.71 us (4%)
  local copies, waits for them, and re-layouts  0.62 us (1%)
    all_to_all x1, blocking collectives, on_device(): lax.all_to_all(jnp.broadcast_to(q[None], (SHARDS, 16, HEAD)), 'kv', split...  13.2 us
    all_to_all x1, blocking collectives, on_device(): lax.all_to_all(partial, 'kv', split_axis=0, concat_axis=0, tiled=True, ax...  11.5 us
    ppermute x1, waiting for transfers between devices, on_device(): return lax.ppermute(mine, axes, [(t, s) for s, t in gather])  8.49 us
    ppermute x1, waiting for transfers between devices, on_device(): q = lax.ppermute(queries.reshape(16, HEAD), axes, gather)  5.39 us
    pallas_call x1, Pallas kernels, on_device(): pl.pallas_call(attend, out_shape=(half, half), in_specs=[vmem, vmem, vmem...  2.75 us
    pallas_call x1, Pallas kernels, on_device(): pl.pallas_call(fetch, out_shape=(jax.ShapeDtypeStruct((EARLY * BLOCK, HEA...  1.84 us
    ppermute x1, starting transfers between devices, on_device(): q = lax.ppermute(queries.reshape(16, HEAD), axes, gather)  1.46 us
    ppermute x1, waiting for transfers between devices, on_device(): got = lax.ppermute(send, 'kv', [(k, k ^ 1) for k in range(SHARDS)])  1.34 us
  transfers between devices with their start and end apart: 3, of which 3 were waited for; matrix products, arithmetic and copies ran while one was open for 0% of the time, Pallas kernels for 4%

profile of v8, /device:TPU:224, one launch (start us, length us, event | category | flops | bytes accessed | tf_op | source)
XLA Modules:
  0.0 47.3 jit_solution(7586201782539448757)
XLA Ops:
  0.0 1.5 %collective-permute-start = (bf16[16,128]{1,0:T(8,128)(2,1)}, bf16[16,128]{1,0:T(8,128)(2,1)S(1)}, u32[]{:S(2)}, u32[]{:S(2)}) collective-permute-start(bf16[16,128]{1,0:T(8,128)(2,1)} %bitcast.10), channel_id=1, source_target_pairs={{0,184},{1,120},{2,56},{3,72},{4,8},{5,200},{6,136},{7,248},{8,176... | collective-permute-start | bytes 12296 | tf_op jit(solution)/shard_map/ppermute | solution.py:227
  1.5 1.8 %fetch.1 = (bf16[10752,128]{1,0:T(8,128)(2,1)S(1)}, bf16[32,128]{1,0:T(8,128)(2,1)S(1)}, bf16[32,128]{1,0:T(8,128)(2,1)S(1)}, s32[2,48]{1,0:T(2,128)S(1)}) custom-call(bf16[12288,128]{1,0:T(8,128)(2,1)} %bitcast.5, bf16[32,128]{1,0:T(8,128)(2,1)} %bitcast.8, bf16[32,128]{1,0:T(8,128)(2,1)} %bitcast.9, s32[2,48]{1,0:T(2,128)} %table_hbm.1, s32[16]{0:T(128)} %lengths_hbm.1), custom_call_target="tpu_custom_call" | custom-call | tf_op jit(solution)/shard_map/fetch/pallas_call | solution.py:237
  3.3 5.4 %collective-permute-done = bf16[16,128]{1,0:T(8,128)(2,1)S(1)} collective-permute-done((bf16[16,128]{1,0:T(8,128)(2,1)}, bf16[16,128]{1,0:T(8,128)(2,1)S(1)}, u32[]{:S(2)}, u32[]{:S(2)}) %collective-permute-start) | collective-permute-done | bytes 4128 | tf_op jit(solution)/shard_map/ppermute | solution.py:227
  8.7 13.2 %all_to_all.10.q_ref = bf16[32,16,128]{2,1,0:T(8,128)(2,1)S(1)} all-to-all(bf16[32,16,128]{2,1,0:T(8,128)(2,1)S(1)} %broadcast_in_dim.2), channel_id=1, replica_groups=mesh['kv'=32,'head'=8] {'kv'}, dimensions={0} | all-to-all | bytes 262144 | tf_op jit(solution)/shard_map/all_to_all | solution.py:256
  21.9 2.8 %attend.1 = (f32[16,24,128]{2,1,0:T(8,128)S(1)}, f32[16,24,128]{2,1,0:T(8,128)S(1)}) custom-call(s32[2,48]{1,0:T(2,128)S(1)} %get-tuple-element.13.plan_vmem, bf16[32,16,128]{2,1,0:T(8,128)(2,1)S(1)} %all_to_all.10.q_ref, bf16[10752,128]{1,0:T(8,128)(2,1)S(1)} %get-tuple-element.16.early_ref, bf16[12288,128]{1,0:T(8,128)(2,1)} %bitcast.6, ...), custom_call_target="tpu_custom_call" | custom-call | tf_op jit(solution)/shard_map/attend/pallas_call | solution.py:260
  24.7 0.2 collective-permute-start.1
  24.9 1.3 %collective-permute-done.1.two_ref = f32[16,24,128]{2,1,0:T(8,128)S(1)} collective-permute-done((f32[16,24,128]{2,1,0:T(8,128)S(1)}, f32[16,24,128]{2,1,0:T(8,128)S(1)}, u32[]{:S(2)}, u32[]{:S(2)}) %collective-permute-start.1) | collective-permute-done | bytes 196640 | tf_op jit(solution)/shard_map/ppermute | solution.py:282
  26.2 0.2 pair.1
  26.4 11.5 %all_to_all.11.in_ref = f32[16,24,128]{2,1,0:T(8,128)S(1)} all-to-all(f32[16,24,128]{2,1,0:T(8,128)S(1)} %pair.1), channel_id=1, replica_groups={{0,16,32,48,64,80,96,112,128,144,160,176,192,208,224,240},{8,24,40,56,7..., dimensions={0} | all-to-all | bytes 393216 | tf_op jit(solution)/shard_map/all_to_all | solution.py:291
  38.0 0.2 combine.1
  38.2 0.1 collective-permute-start.2
  38.2 8.5 %collective-permute-done.2 = f32[4,4,128]{2,1,0:T(4,128)S(1)} collective-permute-done((f32[4,4,128]{2,1,0:T(4,128)S(1)}, f32[4,4,128]{2,1,0:T(4,128)S(1)}, u32[]{:S(2)}, u32[]{:S(2)}) %collective-permute-start.2) | collective-permute-done | bytes 8224 | tf_op jit(solution)/shard_map/ppermute | solution.py:307
  46.7 0.6 %copy.9 = f32[4,4,128]{2,1,0:T(4,128)} copy(f32[4,4,128]{2,1,0:T(4,128)S(1)} %collective-permute-done.2) | data formatting | bytes 16384
  (1 shorter events, 0.0 us)
Async XLA Ops:
  0.0 8.7 %collective-permute-start = (bf16[16,128]{1,0:T(8,128)(2,1)}, bf16[16,128]{1,0:T(8,128)(2,1)S(1)}, u32[]{:S(2)}, u32[]{:S(2)}) collective-permute-start(bf16[16,128]{1,0:T(8,128)(2,1)} %bitcast.10), channel_id=1, source_target_pairs={{0,184},{1,120},{2,56},{3,72},{4,8},{5,200},{6,136},{7,248},{8,176... | collective-permute-start | bytes 12296 | tf_op jit(solution)/shard_map/ppermute | solution.py:227
  24.7 1.5 %collective-permute-start.1 = (f32[16,24,128]{2,1,0:T(8,128)S(1)}, f32[16,24,128]{2,1,0:T(8,128)S(1)}, u32[]{:S(2)}, u32[]{:S(2)}) collective-permute-start(f32[16,24,128]{2,1,0:T(8,128)S(1)} %get-tuple-element.20), channel_id=1, source_target_pairs={{0,8},{8,0},{16,24},{24,16},{32,40},{40,32},{48,56},{56,48},{64,72... | collective-permute-start | bytes 589832 | tf_op jit(solution)/shard_map/ppermute | solution.py:282
  38.2 8.6 %collective-permute-start.2 = (f32[4,4,128]{2,1,0:T(4,128)S(1)}, f32[4,4,128]{2,1,0:T(4,128)S(1)}, u32[]{:S(2)}, u32[]{:S(2)}) collective-permute-start(f32[4,4,128]{2,1,0:T(4,128)S(1)} %combine.1), channel_id=1, source_target_pairs={{184,0},{120,1},{56,2},{72,3},{8,4},{200,5},{136,6},{248,7},{176,8... | collective-permute-start | bytes 24584 | tf_op jit(solution)/shard_map/ppermute | solution.py:307
